TPU v7x, 256 devices: a whole 4x4x8 slice. The times are simulated.
256 devices in a mesh: slab: 16 (over z_hi, y), tp: 4 (over x), band: 4 (over z_lo, core).
Axes of the slice: x: 4, y: 4, z: 8 (z_hi: 4, z_lo: 2; z = z_hi * 2 + z_lo), core: 2. Of those that a mesh axis runs over, the one named last changes fastest.
Arguments:
- tokens: bfloat16 [24576, 3072], P(('slab', 'band'), 'tp'), may hold values from -6 to 6
- w_qkv: bfloat16 [3072, 3, 3072], P('band', None, 'tp'), may hold values from -0.109375 to 0.109375
- w_out: bfloat16 [3072, 3072], P('tp'), may hold values from -0.109375 to 0.109375
- shift: float32 [3072], replicated, may hold values from -3 to 3
- scale: float32 [3072], replicated, may hold values from -0.9 to 0.9
- gate: float32 [3072], P('tp'), may hold values from 0.5 to 2
- q_gain: float32 [128], replicated, may hold values from 0.5 to 5.5
- k_gain: float32 [128], replicated, may hold values from 0.5 to 5.5
- tile_ids: int32 [192, 14], P(('slab', 'band')), may hold values from 0 to 191, as said below
- key_counts: int32 [192], P(('slab', 'band')), may hold values from 1 to 14, as said below
Outputs:
- update: bfloat16 [24576, 3072], P(('slab', 'band'), 'tp')
Inputs may be any that keep to these rules, and one draw needn't show every extreme that they name: `tile_ids`: row q's first key_counts[q] entries are distinct tiles, the first being q itself, whose time index (tile // 12), row index ((tile // 3) % 4) and column index (tile % 3) each differ from q's by at most one; the remaining entries equal q. `key_counts`: 14 is reached in every draw.
All inputs are finite; a program needn't handle non-finite values.
Results may differ from a plain program's by a relative error of at most 0.014.
The roundings to bfloat16 on the way count: a program that leaves them out, or rounds other values in their place, can miss the bound.
Values may be sent and summed in bfloat16 or wider, within the bound.
No kernel may reach another device: no remote copies, remote signals or barrier semaphores. Data moves between devices by JAX's collectives and lax.ppermute only.
A program may use at most 128 MiB of HBM per device.

v0:
```python
import functools

import jax
import jax.numpy as jnp
from jax import lax
from jax.experimental import pallas as pl
from jax.experimental.pallas import tpu as pltpu
from jax.sharding import PartitionSpec as P

HD = 128
HH = 3
HF = HH * HD
TILE = 128
WIN = 14
ROWS = 384
HALF = ROWS // 2
FS = 768
D = 3072
F32 = jnp.float32
BF16 = jnp.bfloat16
HBM = pl.BlockSpec(memory_space=pltpu.HBM)
ANY = pl.BlockSpec(memory_space=pl.ANY)
VM = pl.BlockSpec(memory_space=pltpu.VMEM)
SM = pl.BlockSpec(memory_space=pltpu.SMEM)

RIGHT = [(i, (i + 1) % 4) for i in range(4)]
LEFT = [(i, (i + 3) % 4) for i in range(4)]
ACROSS = [(i, (i + 2) % 4) for i in range(4)]
CORE = [(b, b ^ 1) for b in range(4)]
PAIR = [(b, b ^ 2) for b in range(4)]
LATER = [(i, i + 1) for i in range(15)]
EARLIER = [(i + 1, i) for i in range(15)]


def other_side():
    pairs = []
    for slab in range(16):
        for band in range(4):
            z = (slab // 4) * 2 + band // 2
            z = (z - 1) % 8 if z % 2 == 0 else (z + 1) % 8
            pairs.append((slab * 4 + band, (z // 2 * 4 + slab % 4) * 4 + z % 2 * 2 + band % 2))
    return pairs


OUTER = other_side()


def qkv_kernel(joined, meta, x0, xl, xr, xt, xb, wo, wc, wza, wzb, wca, wcb, scale_in, shift_in, qg_in, kg_in, *rest):
    if joined:
        first, q_ref, kv_ref, both_ref, wbuf, nbuf, xbuf, scale, shift, qg, kg, sems, wsems = rest
    else:
        q_ref, kv_ref, wbuf, nbuf, xbuf, scale, shift, qg, kg, sems, wsems = rest
    far = pl.ds(HALF if joined else 0, HALF)
    early = [(x0, xbuf.at[0]), (xl, xbuf.at[1]), (xr, xbuf.at[2]),
             (xt.at[far], xbuf.at[3, pl.ds(0, HALF)]), (xb.at[far], xbuf.at[3, pl.ds(HALF, HALF)]),
             (scale_in, scale), (shift_in, shift), (qg_in, qg), (kg_in, kg)]

    def krows(k):
        return pl.ds(pl.multiple_of(meta[4 + k] * FS, FS), FS)

    late = [(wo, wbuf.at[:, krows(0)]), (wc, wbuf.at[:, krows(1)]),
            (wza, wbuf.at[0:1, krows(2)]), (wzb, wbuf.at[1:3, krows(2)]),
            (wca, wbuf.at[0:1, krows(3)]), (wcb, wbuf.at[1:3, krows(3)])]
    if joined:
        late.append((first, both_ref.at[pl.ds(0, ROWS)]))
    early = [pltpu.make_async_copy(src, dst, sems.at[n]) for n, (src, dst) in enumerate(early)]
    late = [pltpu.make_async_copy(src, dst, wsems.at[n]) for n, (src, dst) in enumerate(late)]
    for copy in early + late:
        copy.start()
    for copy in early:
        copy.wait()

    step = 32

    def normalise(i, carry):
        r = pl.ds(pl.multiple_of(i * step, step), step)
        parts = [xbuf[k, r, :].astype(F32) for k in range(4)]
        total = functools.reduce(jnp.add, parts)
        center = jnp.sum(total, axis=-1, keepdims=True) * (1.0 / D)
        parts = [p - center for p in parts]
        squares = functools.reduce(jnp.add, [p * p for p in parts])
        inv = lax.rsqrt(jnp.sum(squares, axis=-1, keepdims=True) * (1.0 / D) + 1e-06)
        for k, p in enumerate(parts):
            at = meta[k]
            y = p * inv * (1.0 + scale[at]) + shift[at]
            nbuf[r, pl.ds(pl.multiple_of(at * FS, FS), FS)] = y.astype(BF16)
        return carry

    lax.fori_loop(0, ROWS // step, normalise, 0)
    for copy in late:
        copy.wait()
    for p in (1, 2, 0):
        acc = jnp.dot(nbuf[...], wbuf[p], preferred_element_type=F32)
        if p == 2:
            kv_ref[:, HF:] = acc.astype(BF16)
            continue
        gain = kg if p else qg
        for h in range(HH):
            part = acc[:, h * HD:(h + 1) * HD]
            squares = jnp.mean(part * part, axis=-1, keepdims=True)
            out = (part * lax.rsqrt(squares + 1e-06) * gain[...]).astype(BF16)
            if p:
                kv_ref[:, h * HD:(h + 1) * HD] = out
            else:
                q_ref[:, h * HD:(h + 1) * HD] = out
        if p == 0 and joined:
            both_ref[ROWS:, :] = kv_ref[...]


def qkv(meta, xs, ws, scale, shift, qg, kg, *first):
    shapes = [(ROWS, HF), (ROWS, 2 * HF)] + [(2 * ROWS, 2 * HF)] * len(first)
    return pl.pallas_call(
        functools.partial(qkv_kernel, bool(first)),
        out_shape=[jax.ShapeDtypeStruct(shape, BF16) for shape in shapes],
        in_specs=[SM] + [HBM] * (15 + len(first)),
        out_specs=[VM] * len(shapes),
        scratch_shapes=[
            pltpu.VMEM((3, D, HF), BF16),
            pltpu.VMEM((ROWS, D), BF16),
            pltpu.VMEM((4, ROWS, FS), BF16),
            pltpu.VMEM((4, 1, FS), F32),
            pltpu.VMEM((4, 1, FS), F32),
            pltpu.VMEM((1, HD), F32),
            pltpu.VMEM((1, HD), F32),
            pltpu.SemaphoreType.DMA((9,)),
            pltpu.SemaphoreType.DMA((7,)),
        ],
        compiler_params=pltpu.CompilerParams(vmem_limit_bytes=56 * 2**20),
        cost_estimate=pl.CostEstimate(flops=2 * ROWS * D * 3 * HF, bytes_accessed=10 * 2**20, transcendentals=0),
        name="qkv",
    )(meta, *xs, *ws, scale, shift, qg, kg, *first)


def attend_kernel(meta, ids, q_ref, *rest):
    pieces = rest[:10]
    o_ref, kv, sems = rest[10:]
    y = meta[11]
    jobs = []
    for cr in range(2):
        both, up, down, crossed, direct = pieces[cr * 5:cr * 5 + 5]
        at = [(t * 2 + cr) * 2 * ROWS for t in range(3)]
        jobs.append((None, both, at[1], cr * 5))
        jobs.append((y != 0, up, at[0], cr * 5 + 1))
        jobs.append((y != 3, down, at[2], cr * 5 + 2))
        for last, base in ((0, at[0]), (3, at[2])):
            jobs.append((y == last, crossed, base, cr * 5 + 3))
            jobs.append((y == last, direct, base + ROWS, cr * 5 + 4))

    def each(do):
        for condition, source, first, n in jobs:
            copy = pltpu.make_async_copy(source, kv.at[pl.ds(first, source.shape[0])], sems.at[n])
            if condition is None:
                do(copy)
            else:
                pl.when(condition)(functools.partial(do, copy))

    each(lambda copy: copy.start())
    each(lambda copy: copy.wait())
    slab, side, core = meta[8], meta[9], meta[10]

    def place(tile):
        dt = jnp.clip(tile // 12 - slab + 1, 0, 2)
        row = (tile // 3) % 4
        r = jnp.abs(row // 2 - side)
        cr = jnp.abs(row % 2 - core)
        return (((dt * 2 + cr) * 2 + r) * 3 + tile % 3) * TILE

    factor = 1.0 / HD**0.5

    def run(qt, count, slots):
        spots = [pl.multiple_of(place(ids[qt, j]), TILE) for j in range(slots)]
        rows = pl.ds(pl.multiple_of(qt * TILE, TILE), TILE)
        live = [jnp.where(j < count, 0.0, -1e30) for j in range(slots)]
        cols = [slice(h * HD, (h + 1) * HD) for h in range(HH)]
        vcols = [slice(HF + h * HD, HF + (h + 1) * HD) for h in range(HH)]
        scores = [[] for _ in range(HH)]
        for h in range(HH):
            q = q_ref[rows, cols[h]]
            for j in range(0, slots, 2):
                k = jnp.concatenate([kv[pl.ds(spots[j], TILE), cols[h]], kv[pl.ds(spots[j + 1], TILE), cols[h]]], axis=0)
                s = lax.dot_general(q, k, (((1,), (1,)), ((), ())), preferred_element_type=F32)
                for i in range(2):
                    scores[h].append(s[:, i * TILE:(i + 1) * TILE] * factor + live[j + i])
        tops = [functools.reduce(jnp.maximum, scores[h]) for h in range(HH)]
        tops = [jnp.max(t, axis=-1, keepdims=True) for t in tops]
        weights = [[jnp.exp(s - tops[h]) for s in scores[h]] for h in range(HH)]
        totals = [functools.reduce(jnp.add, weights[h]) for h in range(HH)]
        invs = [1.0 / jnp.sum(t, axis=-1, keepdims=True) for t in totals]
        outs = []
        for h in range(HH):
            acc = None
            for j in range(0, slots, 2):
                p = jnp.concatenate([(w * invs[h]).astype(BF16) for w in weights[h][j:j + 2]], axis=1)
                v = jnp.concatenate([kv[pl.ds(spots[j], TILE), vcols[h]], kv[pl.ds(spots[j + 1], TILE), vcols[h]]], axis=0)
                o = jnp.dot(p, v, preferred_element_type=F32)
                acc = o if acc is None else acc + o
            outs.append(acc.astype(BF16))
        o_ref[rows, :] = jnp.concatenate(outs, axis=1)

    def tile_loop(qt, carry):
        count = ids[qt, WIN]
        lo = 0
        for slots in (4, 8, WIN):
            @pl.when((count > lo) & (count <= slots))
            def _(slots=slots):
                run(qt, count, slots)
            lo = slots
        return carry

    lax.fori_loop(0, ROWS // TILE, tile_loop, 0)


def attend(meta, ids, q, pieces):
    return pl.pallas_call(
        attend_kernel,
        out_shape=jax.ShapeDtypeStruct((ROWS, HF), BF16),
        in_specs=[SM, SM, VM] + [ANY] * 10,
        out_specs=VM,
        scratch_shapes=[
            pltpu.VMEM((12 * ROWS, 2 * HF), BF16),
            pltpu.SemaphoreType.DMA((10,)),
        ],
        compiler_params=pltpu.CompilerParams(vmem_limit_bytes=16 * 2**20),
        cost_estimate=pl.CostEstimate(flops=4 * ROWS * WIN * TILE * HF, bytes_accessed=8 * 2**20,
                                      transcendentals=ROWS * WIN * TILE * HH),
        name="attend",
    )(meta, ids, q, *pieces)


def out_kernel(meta, home, back, w, right_ref, left_ref, keep_right, keep_left, mine_ref):
    side = meta[9]

    def product(k):
        cols = lanes(meta[k], FS)
        rows = [pl.ds(pl.multiple_of(h * HF, HF), HF) for h in (side, 1 - side)]
        return (jnp.dot(home[...], w[rows[0], cols], preferred_element_type=F32)
                + jnp.dot(back[...], w[rows[1], cols], preferred_element_type=F32))

    far = product(3)
    right_ref[:HALF, :] = far[:HALF].astype(BF16)
    left_ref[:HALF, :] = far[HALF:].astype(BF16)
    right = product(2)
    right_ref[HALF:, :] = right[HALF:].astype(BF16)
    keep_right[...] = right[:HALF]
    left = product(1)
    left_ref[HALF:, :] = left[:HALF].astype(BF16)
    keep_left[...] = left[HALF:]
    mine_ref[...] = product(0)


def out_proj(meta, home, back, w):
    return pl.pallas_call(
        out_kernel,
        out_shape=[jax.ShapeDtypeStruct((ROWS, FS), BF16)] * 2 + [jax.ShapeDtypeStruct((HALF, FS), F32)] * 2
        + [jax.ShapeDtypeStruct((ROWS, FS), F32)],
        in_specs=[SM] + [VM] * 3,
        out_specs=[VM] * 5,
        compiler_params=pltpu.CompilerParams(vmem_limit_bytes=24 * 2**20),
        cost_estimate=pl.CostEstimate(flops=2 * ROWS * D * FS, bytes_accessed=8 * 2**20, transcendentals=0),
        name="out_proj",
    )(meta, home, back, w)


def last_kernel(mine, from_left, from_right, left_sum, right_sum, gate, o_ref):
    top = mine[:HALF, :] + from_right[HALF:, :].astype(F32) + left_sum[...].astype(F32)
    o_ref[:HALF, :] = (top * gate[...]).astype(BF16)
    bottom = mine[HALF:, :] + from_left[HALF:, :].astype(F32) + right_sum[...].astype(F32)
    o_ref[HALF:, :] = (bottom * gate[...]).astype(BF16)


def last_sum(*args):
    return pl.pallas_call(
        last_kernel,
        out_shape=jax.ShapeDtypeStruct((ROWS, FS), BF16),
        in_specs=[VM] * 6,
        out_specs=VM,
        compiler_params=pltpu.CompilerParams(vmem_limit_bytes=12 * 2**20),
        name="last_sum",
    )(*args)


def lanes(k, size):
    return pl.ds(pl.multiple_of(k * size, 128), size)


def after(x, *earlier):
    return lax.optimization_barrier((x,) + earlier)[0]


UP = [(s, s + 1) for s in range(15) if s % 4 != 3]
DOWN = [(s + 1, s) for s in range(15) if s % 4 != 3]
WRAP = [(s, s + 1) for s in range(15) if s % 4 == 3] + [(s + 1, s) for s in range(15) if s % 4 == 3]
WRAP_Y = [(s, s - 3) for s in range(15) if s % 4 == 3] + [(s + 1, s + 4) for s in range(15) if s % 4 == 3]
WRAP_Z = [(s - 3, s + 1) for s in range(15) if s % 4 == 3] + [(s + 4, s) for s in range(15) if s % 4 == 3]


def shards(tokens, w_qkv, w_out, shift, scale, gate, q_gain, k_gain, tile_ids, key_counts):
    tp = lax.axis_index("tp")
    slab = lax.axis_index("slab")
    band = lax.axis_index("band")
    side, core = band // 2, band % 2
    meta = jnp.stack([
        tp, (tp + 3) % 4, (tp + 1) % 4, (tp + 2) % 4,
        band, band ^ 1, band ^ 2, band ^ 3,
        slab, side, core, slab % 4,
    ]).astype(jnp.int32)

    swap = functools.partial(lax.ppermute, axis_name="band", perm=CORE)
    pair = functools.partial(lax.ppermute, axis_name="band", perm=PAIR)

    def tp_to(x, perm):
        return lax.ppermute(x, "tp", perm)

    def slab_to(x, perm):
        return lax.ppermute(x, "slab", perm)

    partner_tokens = pair(tokens)
    xl, xr = tp_to(tokens, RIGHT), tp_to(tokens, LEFT)
    w = w_qkv.transpose(1, 0, 2)
    w_own = lax.dynamic_slice_in_dim(w, side * HF, HF, 2)
    w_away = lax.dynamic_slice_in_dim(w, (1 - side) * HF, HF, 2)
    w_zb = lax.ppermute(w_away[1:], ("slab", "band"), OUTER)
    w_za = pair(after(w_away[:1], partner_tokens))
    w_core = swap(w_own)
    passed = after(partner_tokens, xl, xr)
    pl_, pr_ = tp_to(passed, RIGHT), tp_to(passed, LEFT)
    far_top = tp_to(jnp.concatenate([xl[:HALF], pl_[:HALF]], axis=0), RIGHT)
    far_bottom = tp_to(jnp.concatenate([xr[HALF:], pr_[HALF:]], axis=0), LEFT)
    own_x = (tokens, xl, xr, far_top, far_bottom)
    partner_x = (partner_tokens, pl_, pr_, far_top, far_bottom)
    w_za, w_zb = after(w_za, pl_, pr_), after(w_zb, pl_, pr_)
    ws = [w_own, w_core, w_za, w_zb, swap(w_za), swap(w_zb)]

    scale4, shift4 = scale.reshape(4, 1, FS), shift.reshape(4, 1, FS)
    qg, kg = q_gain.reshape(1, HD), k_gain.reshape(1, HD)

    own_q, own_kv = qkv(meta, own_x, ws, scale4, shift4, qg, kg)
    crossed = slab_to(own_kv, WRAP_Y)
    partner_q, partner_kv, both = qkv(meta, partner_x, ws, scale4, shift4, qg, kg, own_kv)
    listed = jnp.concatenate([tile_ids, key_counts[:, None], key_counts[:, None]], axis=1)
    partner_listed = pair(after(listed, own_kv))
    near = [both, slab_to(both, UP), slab_to(after(both, crossed), DOWN),
            slab_to(after(crossed, partner_listed), WRAP_Z), slab_to(partner_kv, WRAP)]
    pieces = near + [swap(x) for x in near]
    away = attend(meta, partner_listed, partner_q, pieces)
    back = pair(away)
    home = attend(meta, listed, after(own_q, away), pieces)
    to_right, to_left, keep_right, keep_left, mine = out_proj(meta, home, back, w_out)
    from_left, from_right = tp_to(to_right, RIGHT), tp_to(to_left, LEFT)
    left_sum = tp_to((keep_right + from_left[:HALF].astype(F32)).astype(BF16), RIGHT)
    right_sum = tp_to((keep_left + from_right[:HALF].astype(F32)).astype(BF16), LEFT)
    return last_sum(mine, from_left, from_right, left_sum, right_sum, gate.reshape(1, FS))


def solution(mesh):
    in_specs = (
        P(("slab", "band"), "tp"),
        P("band", None, "tp"),
        P("tp", None),
        P(),
        P(),
        P("tp"),
        P(),
        P(),
        P(("slab", "band"), None),
        P(("slab", "band")),
    )
    out_specs = P(("slab", "band"), "tp")
    return jax.shard_map(shards, mesh=mesh, in_specs=in_specs, out_specs=out_specs, check_vma=False)
```

profile of v0, /device:TPU:166, one launch (start us, length us, event | category | flops | bytes accessed | tf_op | source)
XLA Modules:
  0.0 174.2 jit_solution(2162468676354780487)
XLA Ops:
  0.0 0.5 collective-permute-start
  0.5 1.5 collective-permute-start.1
  2.0 1.0 collective-permute-start.2
  3.0 2.4 %dynamic-slice_bitcast_fusion = (bf16[3,768,384]{2,1,0:T(8,128)(2,1)S(1)}, bf16[3,768,384]{2,1,0:T(8,128)(2,1)S(1)}) fusion(bf16[768,3,768]{2,0,1:T(8,128)(2,1)} %param.11, s32[]{:T(128)S(6)} %select_n.40, s32[]{:T(128)S(6)} %select_n.39), kind=kLoop, calls=%fused_computation | loop fusion | bytes 7077896 | tf_op jit(solution)/shard_map/dynamic_slice | solution.py:321
  5.4 0.1 slice.37
  5.5 1.1 collective-permute-start.9
  6.7 8.6 %collective-permute-done.xl = bf16[384,768]{1,0:T(8,128)(2,1)S(1)} collective-permute-done((bf16[384,768]{1,0:T(8,128)(2,1)}, bf16[384,768]{1,0:T(8,128)(2,1)S(1)}, u32[]{:S(2)}, u32[]{:S(2)}) %collective-permute-start) | collective-permute-done | bytes 589856 | tf_op jit(solution)/shard_map/ppermute | solution.py:312
  15.3 1.4 collective-permute-done.1.xr
  16.7 0.2 collective-permute-done.2.x0
  16.9 1.7 collective-permute-start.3
  18.5 0.3 collective-permute-start.5
  18.9 0.1 collective-permute-start.7
  19.0 0.1 slice.36
  19.1 0.0 slice-start.3
  19.1 1.1 collective-permute-start.8
  20.2 10.6 %collective-permute-done.3.xl = bf16[384,768]{1,0:T(8,128)(2,1)S(1)} collective-permute-done((bf16[384,768]{1,0:T(8,128)(2,1)}, bf16[384,768]{1,0:T(8,128)(2,1)S(1)}, u32[]{:S(2)}, u32[]{:S(2)}) %collective-permute-start.3) | collective-permute-done | bytes 589856 | tf_op jit(solution)/shard_map/ppermute | solution.py:312
  30.8 2.5 %collective-permute-done.5.xr = bf16[384,768]{1,0:T(8,128)(2,1)S(1)} collective-permute-done((bf16[384,768]{1,0:T(8,128)(2,1)}, bf16[384,768]{1,0:T(8,128)(2,1)S(1)}, u32[]{:S(2)}, u32[]{:S(2)}) %collective-permute-start.5) | collective-permute-done | bytes 589856 | tf_op jit(solution)/shard_map/ppermute | solution.py:312
  33.3 0.0 collective-permute-start.11
  33.3 0.0 slice-start.2
  33.3 0.8 pad_maximum_fusion
  34.2 1.0 collective-permute-start.4
  35.2 0.9 pad_maximum_fusion.1
  36.1 1.0 collective-permute-start.6
  37.1 0.6 stack.51.meta
  37.7 12.5 %collective-permute-done.4.xt = bf16[384,768]{1,0:T(8,128)(2,1)} collective-permute-done((bf16[384,768]{1,0:T(8,128)(2,1)}, bf16[384,768]{1,0:T(8,128)(2,1)}, u32[]{:S(2)}, u32[]{:S(2)}) %collective-permute-start.4) | collective-permute-done | bytes 589856 | tf_op jit(solution)/shard_map/ppermute | solution.py:312
  50.2 2.9 %collective-permute-done.6.xb = bf16[384,768]{1,0:T(8,128)(2,1)} collective-permute-done((bf16[384,768]{1,0:T(8,128)(2,1)}, bf16[384,768]{1,0:T(8,128)(2,1)}, u32[]{:S(2)}, u32[]{:S(2)}) %collective-permute-start.6) | collective-permute-done | bytes 589856 | tf_op jit(solution)/shard_map/ppermute | solution.py:312
  53.1 1.2 copy-done.5
  54.3 11.4 %qkv.2 = (bf16[384,384]{1,0:T(8,128)(2,1)}, bf16[384,768]{1,0:T(8,128)(2,1)}) custom-call(s32[12]{0:T(128)} %stack.51.meta, bf16[384,768]{1,0:T(8,128)(2,1)} %x0.1, bf16[384,768]{1,0:T(8,128)(2,1)} %copy-done.9, bf16[384,768]{1,0:T(8,128)(2,1)} %copy-done.8, bf16[384,768]{1,0:T(8,128)(2,1)} %collective-permute-done.4.xt, ...), custom_call_target="tpu_custom_call" | custom-call | flops 2717908992 | bytes 10485760 | tf_op jit(solution)/shard_map/qkv/pallas_call | solution.py:112
  65.7 0.0 copy-start.12
  65.7 0.0 copy-start.11
  65.7 5.1 %collective-permute-start.14 = (bf16[384,768]{1,0:T(8,128)(2,1)}, bf16[384,768]{1,0:T(8,128)(2,1)S(1)}, u32[]{:S(2)}, u32[]{:S(2)}) collective-permute-start(bf16[384,768]{1,0:T(8,128)(2,1)} %get-tuple-element.28.rest_0_), channel_id=1, source_target_pairs={{48,0},{112,64},{176,128},{64,112},{128,176},{192,240},{49,1},{113... | collective-permute-start | bytes 1769480 | tf_op jit(solution)/shard_map/ppermute | solution.py:315
  70.9 12.0 %qkv.3 = (bf16[384,384]{1,0:T(8,128)(2,1)}, bf16[384,768]{1,0:T(8,128)(2,1)}, bf16[768,768]{1,0:T(8,128)(2,1)}) custom-call(s32[12]{0:T(128)} %stack.51.meta, bf16[384,768]{1,0:T(8,128)(2,1)} %collective-permute-done.2.x0, bf16[384,768]{1,0:T(8,128)(2,1)} %copy-done.6, bf16[384,768]{1,0:T(8,128)(2,1)} %copy-done.7, ...), custom_call_target="tpu_custom_call" | custom-call | flops 2717908992 | bytes 10485760 | tf_op jit(solution)/shard_map/qkv/pallas_call | solution.py:112
  82.9 1.4 collective-permute-start.13
  84.3 1.3 collective-permute-start.15
  85.6 0.1 copy.11
  85.7 0.1 pad_add_fusion.ids
  85.8 2.3 %collective-permute-start.12 = (s32[3,16]{1,0:T(4,128)S(1)}, s32[3,16]{1,0:T(4,128)S(1)}, u32[]{:S(2)}, u32[]{:S(2)}) collective-permute-start(s32[3,16]{1,0:T(4,128)S(1)} %pad_add_fusion.ids), channel_id=1, source_target_pairs={{0,2},{1,3},{2,0},{3,1},{4,6},{5,7},{6,4},{7,5},{8,10},{9,11},{10,... | collective-permute-start | bytes 584 | tf_op jit(solution)/shard_map/ppermute | solution.py:341
  88.0 4.7 %collective-permute-start.17 = (bf16[384,768]{1,0:T(8,128)(2,1)}, bf16[384,768]{1,0:T(8,128)(2,1)S(1)}, u32[]{:S(2)}, u32[]{:S(2)}) collective-permute-start(bf16[384,768]{1,0:T(8,128)(2,1)} %get-tuple-element.34), channel_id=1, source_target_pairs={{48,64},{112,128},{176,192},{64,48},{128,112},{192,176},{49,65},{1... | collective-permute-start | bytes 1769480 | tf_op jit(solution)/shard_map/ppermute | solution.py:315
  92.7 5.0 %collective-permute-start.16 = (bf16[384,768]{1,0:T(8,128)(2,1)S(1)}, bf16[384,768]{1,0:T(8,128)(2,1)S(1)}, u32[]{:S(2)}, u32[]{:S(2)}) collective-permute-start(bf16[384,768]{1,0:T(8,128)(2,1)S(1)} %collective-permute-done.14), channel_id=1, source_target_pairs={{0,64},{64,128},{128,192},{112,48},{176,112},{240,176},{1,65},{65,... | collective-permute-start | bytes 1769480 | tf_op jit(solution)/shard_map/ppermute | solution.py:315
  97.7 11.6 %collective-permute-done.13.rest_1_ = bf16[768,768]{1,0:T(8,128)(2,1)S(1)} collective-permute-done((bf16[768,768]{1,0:T(8,128)(2,1)}, bf16[768,768]{1,0:T(8,128)(2,1)S(1)}, u32[]{:S(2)}, u32[]{:S(2)}) %collective-permute-start.13) | collective-permute-done | bytes 1179680 | tf_op jit(solution)/shard_map/ppermute | solution.py:315
  109.3 4.1 %collective-permute-done.15.rest_2_ = bf16[768,768]{1,0:T(8,128)(2,1)S(1)} collective-permute-done((bf16[768,768]{1,0:T(8,128)(2,1)}, bf16[768,768]{1,0:T(8,128)(2,1)S(1)}, u32[]{:S(2)}, u32[]{:S(2)}) %collective-permute-start.15) | collective-permute-done | bytes 1179680 | tf_op jit(solution)/shard_map/ppermute | solution.py:315
  113.4 8.9 %collective-permute-done.17.rest_4_ = bf16[384,768]{1,0:T(8,128)(2,1)S(1)} collective-permute-done((bf16[384,768]{1,0:T(8,128)(2,1)}, bf16[384,768]{1,0:T(8,128)(2,1)S(1)}, u32[]{:S(2)}, u32[]{:S(2)}) %collective-permute-start.17) | collective-permute-done | bytes 589856 | tf_op jit(solution)/shard_map/ppermute | solution.py:315
  122.2 0.1 collective-permute-start.22
  122.3 1.5 collective-permute-done.16.rest_3_
  123.8 0.4 collective-permute-done.22.rest_9_
  124.3 1.6 collective-permute-done.21.rest_8_
  125.9 1.3 copy-done
  127.1 1.0 copy-done.2
  128.1 5.7 %attend.2 = bf16[384,384]{1,0:T(8,128)(2,1)S(1)} custom-call(s32[12]{0:T(128)S(1)} %copy-done.3, s32[3,16]{1,0:T(4,128)S(1)} %collective-permute-done.12.ids, bf16[384,384]{1,0:T(8,128)(2,1)S(1)} %copy-done.2, bf16[768,768]{1,0:T(8,128)(2,1)S(1)} %copy-done, bf16[768,768]{1,0:T(8,128)(2,1)S(1)} %collective-permute-done.13.rest_1_, ...), custom_call_target="tpu_custom_call" | custom-call | flops 1056964608 | bytes 8388608 | tf_op jit(solution)/shard_map/attend/pallas_call | solution.py:214
  133.8 0.0 slice-start.1
  133.8 2.4 %collective-permute-start.23 = (bf16[384,384]{1,0:T(8,128)(2,1)S(1)}, bf16[384,384]{1,0:T(8,128)(2,1)S(1)}, u32[]{:S(2)}, u32[]{:S(2)}) collective-permute-start(bf16[384,384]{1,0:T(8,128)(2,1)S(1)} %attend.2), channel_id=1, source_target_pairs={{0,2},{1,3},{2,0},{3,1},{4,6},{5,7},{6,4},{7,5},{8,10},{9,11},{10,... | collective-permute-start | bytes 884744 | tf_op jit(solution)/shard_map/ppermute | solution.py:346
  136.2 5.4 %attend.3.home = bf16[384,384]{1,0:T(8,128)(2,1)S(1)} custom-call(s32[12]{0:T(128)S(1)} %copy-done.3, s32[3,16]{1,0:T(4,128)S(1)} %pad_add_fusion.ids, bf16[384,384]{1,0:T(8,128)(2,1)S(1)} %copy-done.1, bf16[768,768]{1,0:T(8,128)(2,1)S(1)} %copy-done, bf16[768,768]{1,0:T(8,128)(2,1)S(1)} %collective-permute-done.13.rest_1_, ...), custom_call_target="tpu_custom_call" | custom-call | flops 1056964608 | bytes 8388608 | tf_op jit(solution)/shard_map/attend/pallas_call | solution.py:214
  141.5 2.3 %collective-permute-done.23.back = bf16[384,384]{1,0:T(8,128)(2,1)S(1)} collective-permute-done((bf16[384,384]{1,0:T(8,128)(2,1)S(1)}, bf16[384,384]{1,0:T(8,128)(2,1)S(1)}, u32[]{:S(2)}, u32[]{:S(2)}) %collective-permute-start.23) | collective-permute-done | bytes 294944 | tf_op jit(solution)/shard_map/ppermute | solution.py:346
  143.8 3.2 %out_proj.1 = (bf16[384,768]{1,0:T(8,128)(2,1)S(1)}, bf16[384,768]{1,0:T(8,128)(2,1)S(1)}, f32[192,768]{1,0:T(8,128)S(1)}, f32[192,768]{1,0:T(8,128)S(1)}, f32[384,768]{1,0:T(8,128)S(1)}) custom-call(s32[12]{0:T(128)S(1)} %copy-done.3, bf16[384,384]{1,0:T(8,128)(2,1)S(1)} %attend.3.home, bf16[384,384]{1,0:T(8,128)(2,1)S(1)} %collective-permute-done.23.back, ...), custom_call_target="tpu_custom_call" | custom-call | flops 1811939328 | bytes 8388608 | tf_op jit(solution)/shard_map/out_proj/pallas_call | solution.py:252
  147.0 0.1 collective-permute-start.24
  147.1 2.0 %collective-permute-start.25 = (bf16[384,768]{1,0:T(8,128)(2,1)S(1)}, bf16[384,768]{1,0:T(8,128)(2,1)S(1)}, u32[]{:S(2)}, u32[]{:S(2)}) collective-permute-start(bf16[384,768]{1,0:T(8,128)(2,1)S(1)} %get-tuple-element.38), channel_id=1, source_target_pairs={{0,12},{4,0},{8,4},{12,8},{1,13},{5,1},{9,5},{13,9},{2,14},{6,2},{... | collective-permute-start | bytes 1769480 | tf_op jit(solution)/shard_map/ppermute | solution.py:312
  149.1 13.1 %collective-permute-done.24.from_left = bf16[384,768]{1,0:T(8,128)(2,1)S(1)} collective-permute-done((bf16[384,768]{1,0:T(8,128)(2,1)S(1)}, bf16[384,768]{1,0:T(8,128)(2,1)S(1)}, u32[]{:S(2)}, u32[]{:S(2)}) %collective-permute-start.24) | collective-permute-done | bytes 589856 | tf_op jit(solution)/shard_map/ppermute | solution.py:312
  162.2 0.1 add_convert_fusion.1
  162.3 1.6 collective-permute-start.26
  163.8 0.1 add_convert_fusion
  163.9 0.6 collective-permute-start.27
  164.5 5.8 %collective-permute-done.26.left_sum = bf16[192,768]{1,0:T(8,128)(2,1)S(1)} collective-permute-done((bf16[192,768]{1,0:T(8,128)(2,1)S(1)}, bf16[192,768]{1,0:T(8,128)(2,1)S(1)}, u32[]{:S(2)}, u32[]{:S(2)}) %collective-permute-start.26) | collective-permute-done | bytes 294944 | tf_op jit(solution)/shard_map/ppermute | solution.py:312
  170.3 2.9 %collective-permute-done.27.right_sum = bf16[192,768]{1,0:T(8,128)(2,1)S(1)} collective-permute-done((bf16[192,768]{1,0:T(8,128)(2,1)S(1)}, bf16[192,768]{1,0:T(8,128)(2,1)S(1)}, u32[]{:S(2)}, u32[]{:S(2)}) %collective-permute-start.27) | collective-permute-done | bytes 294944 | tf_op jit(solution)/shard_map/ppermute | solution.py:312
  173.2 1.1 last_sum.1
  (46 shorter events, 0.1 us)
Async XLA Ops:
  0.0 15.3 %collective-permute-start = (bf16[384,768]{1,0:T(8,128)(2,1)}, bf16[384,768]{1,0:T(8,128)(2,1)S(1)}, u32[]{:S(2)}, u32[]{:S(2)}) collective-permute-start(bf16[384,768]{1,0:T(8,128)(2,1)} %x0.1), channel_id=1, source_target_pairs={{0,4},{4,8},{8,12},{12,0},{1,5},{5,9},{9,13},{13,1},{2,6},{6,10},{... | collective-permute-start | bytes 1769480 | tf_op jit(solution)/shard_map/ppermute | solution.py:312
  0.5 16.2 %collective-permute-start.1 = (bf16[384,768]{1,0:T(8,128)(2,1)}, bf16[384,768]{1,0:T(8,128)(2,1)S(1)}, u32[]{:S(2)}, u32[]{:S(2)}) collective-permute-start(bf16[384,768]{1,0:T(8,128)(2,1)} %x0.1), channel_id=1, source_target_pairs={{0,12},{4,0},{8,4},{12,8},{1,13},{5,1},{9,5},{13,9},{2,14},{6,2},{... | collective-permute-start | bytes 1769480 | tf_op jit(solution)/shard_map/ppermute | solution.py:312
  2.0 14.8 %collective-permute-start.2 = (bf16[384,768]{1,0:T(8,128)(2,1)}, bf16[384,768]{1,0:T(8,128)(2,1)}, u32[]{:S(2)}, u32[]{:S(2)}) collective-permute-start(bf16[384,768]{1,0:T(8,128)(2,1)} %x0.1), channel_id=1, source_target_pairs={{0,2},{1,3},{2,0},{3,1},{4,6},{5,7},{6,4},{7,5},{8,10},{9,11},{10,... | collective-permute-start | bytes 1769480 | tf_op jit(solution)/shard_map/ppermute | solution.py:317
  5.4 13.5 %copy-start.4 = (bf16[3,768,384]{2,1,0:T(8,128)(2,1)}, bf16[3,768,384]{2,1,0:T(8,128)(2,1)S(1)}, u32[]{:S(2)}) copy-start(bf16[3,768,384]{2,1,0:T(8,128)(2,1)S(1)} %get-tuple-element.42.wo) | copy-start | bytes 5308420
  5.5 27.7 %collective-permute-start.9 = (bf16[2,768,384]{2,1,0:T(8,128)(2,1)S(1)}, bf16[2,768,384]{2,1,0:T(8,128)(2,1)}, u32[]{:S(2)}, u32[]{:S(2)}) collective-permute-start(bf16[2,768,384]{2,1,0:T(8,128)(2,1)S(1)} %slice.37), channel_id=1, source_target_pairs={{0,194},{1,195},{2,64},{3,65},{16,210},{17,211},{18,80},{19,81},{3... | collective-permute-start | bytes 3538952 | tf_op jit(solution)/shard_map/ppermute | solution.py:322
  15.3 3.6 %copy-start.9 = (bf16[384,768]{1,0:T(8,128)(2,1)}, bf16[384,768]{1,0:T(8,128)(2,1)S(1)}, u32[]{:S(2)}) copy-start(bf16[384,768]{1,0:T(8,128)(2,1)S(1)} %collective-permute-done.xl) | copy-start | bytes 1769476
  16.7 2.2 %copy-start.8 = (bf16[384,768]{1,0:T(8,128)(2,1)}, bf16[384,768]{1,0:T(8,128)(2,1)S(1)}, u32[]{:S(2)}) copy-start(bf16[384,768]{1,0:T(8,128)(2,1)S(1)} %collective-permute-done.1.xr) | copy-start | bytes 1769476
  16.9 13.9 %collective-permute-start.3 = (bf16[384,768]{1,0:T(8,128)(2,1)}, bf16[384,768]{1,0:T(8,128)(2,1)S(1)}, u32[]{:S(2)}, u32[]{:S(2)}) collective-permute-start(bf16[384,768]{1,0:T(8,128)(2,1)} %collective-permute-done.2.x0), channel_id=1, source_target_pairs={{0,4},{4,8},{8,12},{12,0},{1,5},{5,9},{9,13},{13,1},{2,6},{6,10},{... | collective-permute-start | bytes 1769480 | tf_op jit(solution)/shard_map/ppermute | solution.py:312
  18.5 14.7 %collective-permute-start.5 = (bf16[384,768]{1,0:T(8,128)(2,1)}, bf16[384,768]{1,0:T(8,128)(2,1)S(1)}, u32[]{:S(2)}, u32[]{:S(2)}) collective-permute-start(bf16[384,768]{1,0:T(8,128)(2,1)} %collective-permute-done.2.x0), channel_id=1, source_target_pairs={{0,12},{4,0},{8,4},{12,8},{1,13},{5,1},{9,5},{13,9},{2,14},{6,2},{... | collective-permute-start | bytes 1769480 | tf_op jit(solution)/shard_map/ppermute | solution.py:312
  18.9 34.2 %collective-permute-start.7 = (bf16[3,768,384]{2,1,0:T(8,128)(2,1)S(1)}, bf16[3,768,384]{2,1,0:T(8,128)(2,1)S(1)}, u32[]{:S(2)}, u32[]{:S(2)}) collective-permute-start(bf16[3,768,384]{2,1,0:T(8,128)(2,1)S(1)} %get-tuple-element.42.wo), channel_id=1, source_target_pairs={{0,1},{1,0},{2,3},{3,2},{4,5},{5,4},{6,7},{7,6},{8,9},{9,8},{10,11... | collective-permute-start | bytes 5308424 | tf_op jit(solution)/shard_map/ppermute | solution.py:324
  19.1 14.3 %slice-start.3 = ((bf16[384,768]{1,0:T(8,128)(2,1)}), bf16[192,768]{1,0:T(8,128)(2,1)S(1)}, s32[]{:S(2)}) async-start(bf16[384,768]{1,0:T(8,128)(2,1)} %copy-done.9), calls=%async_computation.3 | async-start | bytes 589824 | tf_op jit(solution)/shard_map/slice | solution.py:327
  19.1 18.0 %collective-permute-start.8 = (bf16[1,768,384]{2,1,0:T(8,128)(2,1)S(1)}, bf16[1,768,384]{2,1,0:T(8,128)(2,1)}, u32[]{:S(2)}, u32[]{:S(2)}) collective-permute-start(bf16[1,768,384]{2,1,0:T(8,128)(2,1)S(1)} %slice.36), channel_id=1, source_target_pairs={{0,2},{1,3},{2,0},{3,1},{4,6},{5,7},{6,4},{7,5},{8,10},{9,11},{10,... | collective-permute-start | bytes 1769480 | tf_op jit(solution)/shard_map/ppermute | solution.py:323
  30.8 3.4 %copy-start.6 = (bf16[384,768]{1,0:T(8,128)(2,1)}, bf16[384,768]{1,0:T(8,128)(2,1)S(1)}, u32[]{:S(2)}) copy-start(bf16[384,768]{1,0:T(8,128)(2,1)S(1)} %collective-permute-done.3.xl) | copy-start | bytes 1769476
  33.3 1.9 %copy-start.7 = (bf16[384,768]{1,0:T(8,128)(2,1)}, bf16[384,768]{1,0:T(8,128)(2,1)S(1)}, u32[]{:S(2)}) copy-start(bf16[384,768]{1,0:T(8,128)(2,1)S(1)} %collective-permute-done.5.xr) | copy-start | bytes 1769476
  33.3 19.8 %collective-permute-start.11 = (bf16[2,768,384]{2,1,0:T(8,128)(2,1)}, bf16[2,768,384]{2,1,0:T(8,128)(2,1)}, u32[]{:S(2)}, u32[]{:S(2)}) collective-permute-start(bf16[2,768,384]{2,1,0:T(8,128)(2,1)} %collective-permute-done.9.wzb), channel_id=1, source_target_pairs={{0,1},{1,0},{2,3},{3,2},{4,5},{5,4},{6,7},{7,6},{8,9},{9,8},{10,11... | collective-permute-start | bytes 3538952 | tf_op jit(solution)/shard_map/ppermute | solution.py:332
  33.3 1.9 %slice-start.2 = ((bf16[384,768]{1,0:T(8,128)(2,1)}), bf16[192,768]{1,0:T(8,128)(2,1)S(1)}, s32[]{:S(2)}) async-start(bf16[384,768]{1,0:T(8,128)(2,1)} %copy-done.8), calls=%async_computation.2 | async-start | bytes 589824 | tf_op jit(solution)/shard_map/slice | solution.py:328
  34.2 16.0 %collective-permute-start.4 = (bf16[384,768]{1,0:T(8,128)(2,1)}, bf16[384,768]{1,0:T(8,128)(2,1)}, u32[]{:S(2)}, u32[]{:S(2)}) collective-permute-start(bf16[384,768]{1,0:T(8,128)(2,1)} %pad_maximum_fusion), channel_id=1, source_target_pairs={{0,4},{4,8},{8,12},{12,0},{1,5},{5,9},{9,13},{13,1},{2,6},{6,10},{... | collective-permute-start | bytes 1769480 | tf_op jit(solution)/shard_map/ppermute | solution.py:312
  36.1 17.0 %collective-permute-start.6 = (bf16[384,768]{1,0:T(8,128)(2,1)}, bf16[384,768]{1,0:T(8,128)(2,1)}, u32[]{:S(2)}, u32[]{:S(2)}) collective-permute-start(bf16[384,768]{1,0:T(8,128)(2,1)} %pad_maximum_fusion.1), channel_id=1, source_target_pairs={{0,12},{4,0},{8,4},{12,8},{1,13},{5,1},{9,5},{13,9},{2,14},{6,2},{... | collective-permute-start | bytes 1769480 | tf_op jit(solution)/shard_map/ppermute | solution.py:312
  37.1 16.0 %collective-permute-start.10 = (bf16[1,768,384]{2,1,0:T(8,128)(2,1)}, bf16[1,768,384]{2,1,0:T(8,128)(2,1)}, u32[]{:S(2)}, u32[]{:S(2)}) collective-permute-start(bf16[1,768,384]{2,1,0:T(8,128)(2,1)} %collective-permute-done.8.wza), channel_id=1, source_target_pairs={{0,1},{1,0},{2,3},{3,2},{4,5},{5,4},{6,7},{7,6},{8,9},{9,8},{10,11... | collective-permute-start | bytes 1769480 | tf_op jit(solution)/shard_map/ppermute | solution.py:332
  53.1 1.2 copy-start.5
  65.7 19.9 %copy-start.12 = (s32[3]{0:T(128)S(1)}, s32[3]{0:T(128)}, u32[]{:S(2)}) copy-start(s32[3]{0:T(128)} %param.19) | copy-start | bytes 40
  65.7 20.0 %copy-start.11 = (s32[3,14]{1,0:T(4,128)S(1)}, s32[3,14]{1,0:T(4,128)}, u32[]{:S(2)}) copy-start(s32[3,14]{1,0:T(4,128)} %param.18) | copy-start | bytes 508
  65.7 60.1 %copy-start.3 = (s32[12]{0:T(128)S(1)}, s32[12]{0:T(128)}, u32[]{:S(2)}) copy-start(s32[12]{0:T(128)} %stack.51.meta) | copy-start | bytes 148
  65.7 18.5 %collective-permute-start.14 = (bf16[384,768]{1,0:T(8,128)(2,1)}, bf16[384,768]{1,0:T(8,128)(2,1)S(1)}, u32[]{:S(2)}, u32[]{:S(2)}) collective-permute-start(bf16[384,768]{1,0:T(8,128)(2,1)} %get-tuple-element.28.rest_0_), channel_id=1, source_target_pairs={{48,0},{112,64},{176,128},{64,112},{128,176},{192,240},{49,1},{113... | collective-permute-start | bytes 1769480 | tf_op jit(solution)/shard_map/ppermute | solution.py:315
  82.9 26.4 %collective-permute-start.13 = (bf16[768,768]{1,0:T(8,128)(2,1)}, bf16[768,768]{1,0:T(8,128)(2,1)S(1)}, u32[]{:S(2)}, u32[]{:S(2)}) collective-permute-start(bf16[768,768]{1,0:T(8,128)(2,1)} %get-tuple-element.32.rest_0_), channel_id=1, source_target_pairs={{0,16},{16,32},{32,48},{64,80},{80,96},{96,112},{128,144},{144,160... | collective-permute-start | bytes 3538952 | tf_op jit(solution)/shard_map/ppermute | solution.py:315
  84.3 29.1 %collective-permute-start.15 = (bf16[768,768]{1,0:T(8,128)(2,1)}, bf16[768,768]{1,0:T(8,128)(2,1)S(1)}, u32[]{:S(2)}, u32[]{:S(2)}) collective-permute-start(bf16[768,768]{1,0:T(8,128)(2,1)} %get-tuple-element.32.rest_0_), channel_id=1, source_target_pairs={{16,0},{32,16},{48,32},{80,64},{96,80},{112,96},{144,128},{160,144... | collective-permute-start | bytes 3538952 | tf_op jit(solution)/shard_map/ppermute | solution.py:315
  85.8 6.9 %collective-permute-start.12 = (s32[3,16]{1,0:T(4,128)S(1)}, s32[3,16]{1,0:T(4,128)S(1)}, u32[]{:S(2)}, u32[]{:S(2)}) collective-permute-start(s32[3,16]{1,0:T(4,128)S(1)} %pad_add_fusion.ids), channel_id=1, source_target_pairs={{0,2},{1,3},{2,0},{3,1},{4,6},{5,7},{6,4},{7,5},{8,10},{9,11},{10,... | collective-permute-start | bytes 584 | tf_op jit(solution)/shard_map/ppermute | solution.py:341
  88.0 35.8 %collective-permute-start.18 = (bf16[768,768]{1,0:T(8,128)(2,1)}, bf16[768,768]{1,0:T(8,128)(2,1)S(1)}, u32[]{:S(2)}, u32[]{:S(2)}) collective-permute-start(bf16[768,768]{1,0:T(8,128)(2,1)} %get-tuple-element.32.rest_0_), channel_id=1, source_target_pairs={{0,1},{1,0},{2,3},{3,2},{4,5},{5,4},{6,7},{7,6},{8,9},{9,8},{10,11... | collective-permute-start | bytes 3538952 | tf_op jit(solution)/shard_map/ppermute | solution.py:344
  88.0 34.2 %collective-permute-start.17 = (bf16[384,768]{1,0:T(8,128)(2,1)}, bf16[384,768]{1,0:T(8,128)(2,1)S(1)}, u32[]{:S(2)}, u32[]{:S(2)}) collective-permute-start(bf16[384,768]{1,0:T(8,128)(2,1)} %get-tuple-element.34), channel_id=1, source_target_pairs={{48,64},{112,128},{176,192},{64,48},{128,112},{192,176},{49,65},{1... | collective-permute-start | bytes 1769480 | tf_op jit(solution)/shard_map/ppermute | solution.py:315
  92.7 31.1 %collective-permute-start.16 = (bf16[384,768]{1,0:T(8,128)(2,1)S(1)}, bf16[384,768]{1,0:T(8,128)(2,1)S(1)}, u32[]{:S(2)}, u32[]{:S(2)}) collective-permute-start(bf16[384,768]{1,0:T(8,128)(2,1)S(1)} %collective-permute-done.14), channel_id=1, source_target_pairs={{0,64},{64,128},{128,192},{112,48},{176,112},{240,176},{1,65},{65,... | collective-permute-start | bytes 1769480 | tf_op jit(solution)/shard_map/ppermute | solution.py:315
  109.3 16.6 %collective-permute-start.19 = (bf16[768,768]{1,0:T(8,128)(2,1)S(1)}, bf16[768,768]{1,0:T(8,128)(2,1)S(1)}, u32[]{:S(2)}, u32[]{:S(2)}) collective-permute-start(bf16[768,768]{1,0:T(8,128)(2,1)S(1)} %collective-permute-done.13.rest_1_), channel_id=1, source_target_pairs={{0,1},{1,0},{2,3},{3,2},{4,5},{5,4},{6,7},{7,6},{8,9},{9,8},{10,11... | collective-permute-start | bytes 3538952 | tf_op jit(solution)/shard_map/ppermute | solution.py:344
  113.4 12.5 %collective-permute-start.20 = (bf16[768,768]{1,0:T(8,128)(2,1)S(1)}, bf16[768,768]{1,0:T(8,128)(2,1)S(1)}, u32[]{:S(2)}, u32[]{:S(2)}) collective-permute-start(bf16[768,768]{1,0:T(8,128)(2,1)S(1)} %collective-permute-done.15.rest_2_), channel_id=1, source_target_pairs={{0,1},{1,0},{2,3},{3,2},{4,5},{5,4},{6,7},{7,6},{8,9},{9,8},{10,11... | collective-permute-start | bytes 3538952 | tf_op jit(solution)/shard_map/ppermute | solution.py:344
  122.2 2.0 %collective-permute-start.22 = (bf16[384,768]{1,0:T(8,128)(2,1)S(1)}, bf16[384,768]{1,0:T(8,128)(2,1)S(1)}, u32[]{:S(2)}, u32[]{:S(2)}) collective-permute-start(bf16[384,768]{1,0:T(8,128)(2,1)S(1)} %collective-permute-done.17.rest_4_), channel_id=1, source_target_pairs={{0,1},{1,0},{2,3},{3,2},{4,5},{5,4},{6,7},{7,6},{8,9},{9,8},{10,11... | collective-permute-start | bytes 1769480 | tf_op jit(solution)/shard_map/ppermute | solution.py:344
  123.8 2.0 %collective-permute-start.21 = (bf16[384,768]{1,0:T(8,128)(2,1)S(1)}, bf16[384,768]{1,0:T(8,128)(2,1)S(1)}, u32[]{:S(2)}, u32[]{:S(2)}) collective-permute-start(bf16[384,768]{1,0:T(8,128)(2,1)S(1)} %collective-permute-done.16.rest_3_), channel_id=1, source_target_pairs={{0,1},{1,0},{2,3},{3,2},{4,5},{5,4},{6,7},{7,6},{8,9},{9,8},{10,11... | collective-permute-start | bytes 1769480 | tf_op jit(solution)/shard_map/ppermute | solution.py:344
  125.9 1.3 copy-start
  127.1 1.0 copy-start.2
  128.1 8.1 %copy-start.1 = (bf16[384,384]{1,0:T(8,128)(2,1)S(1)}, bf16[384,384]{1,0:T(8,128)(2,1)}, u32[]{:S(2)}) copy-start(bf16[384,384]{1,0:T(8,128)(2,1)} %get-tuple-element.35.q_ref) | copy-start | bytes 884740
  128.1 15.7 %slice-start = ((s8[4718592]{0:T(1024)(128)(4,1)}), s8[4194304]{0:T(1024)(128)(4,1)S(1)}, s32[]{:S(2)}) async-start(s8[4718592]{0:T(1024)(128)(4,1)} %bitcast.21), calls=%async_computation | async-start | bytes 8388608
  133.8 10.0 %slice-start.1 = ((s8[4718592]{0:T(1024)(128)(4,1)}), s8[524288]{0:T(1024)(128)(4,1)S(1)}, s32[]{:S(2)}) async-start(s8[4718592]{0:T(1024)(128)(4,1)} %bitcast.21), calls=%async_computation.1 | async-start | bytes 1048576
  133.8 10.0 %collective-permute-start.23 = (bf16[384,384]{1,0:T(8,128)(2,1)S(1)}, bf16[384,384]{1,0:T(8,128)(2,1)S(1)}, u32[]{:S(2)}, u32[]{:S(2)}) collective-permute-start(bf16[384,384]{1,0:T(8,128)(2,1)S(1)} %attend.2), channel_id=1, source_target_pairs={{0,2},{1,3},{2,0},{3,1},{4,6},{5,7},{6,4},{7,5},{8,10},{9,11},{10,... | collective-permute-start | bytes 884744 | tf_op jit(solution)/shard_map/ppermute | solution.py:346
  147.0 15.2 %collective-permute-start.24 = (bf16[384,768]{1,0:T(8,128)(2,1)S(1)}, bf16[384,768]{1,0:T(8,128)(2,1)S(1)}, u32[]{:S(2)}, u32[]{:S(2)}) collective-permute-start(bf16[384,768]{1,0:T(8,128)(2,1)S(1)} %get-tuple-element.37), channel_id=1, source_target_pairs={{0,4},{4,8},{8,12},{12,0},{1,5},{5,9},{9,13},{13,1},{2,6},{6,10},{... | collective-permute-start | bytes 1769480 | tf_op jit(solution)/shard_map/ppermute | solution.py:312
  147.1 16.8 %collective-permute-start.25 = (bf16[384,768]{1,0:T(8,128)(2,1)S(1)}, bf16[384,768]{1,0:T(8,128)(2,1)S(1)}, u32[]{:S(2)}, u32[]{:S(2)}) collective-permute-start(bf16[384,768]{1,0:T(8,128)(2,1)S(1)} %get-tuple-element.38), channel_id=1, source_target_pairs={{0,12},{4,0},{8,4},{12,8},{1,13},{5,1},{9,5},{13,9},{2,14},{6,2},{... | collective-permute-start | bytes 1769480 | tf_op jit(solution)/shard_map/ppermute | solution.py:312
  162.2 2.3 %copy-start.10 = (f32[768]{0:T(1024)S(1)}, f32[768]{0:T(1024)}, u32[]{:S(2)}) copy-start(f32[768]{0:T(1024)} %param.15) | copy-start | bytes 9220
  162.3 8.0 %collective-permute-start.26 = (bf16[192,768]{1,0:T(8,128)(2,1)S(1)}, bf16[192,768]{1,0:T(8,128)(2,1)S(1)}, u32[]{:S(2)}, u32[]{:S(2)}) collective-permute-start(bf16[192,768]{1,0:T(8,128)(2,1)S(1)} %add_convert_fusion.1), channel_id=1, source_target_pairs={{0,4},{4,8},{8,12},{12,0},{1,5},{5,9},{9,13},{13,1},{2,6},{6,10},{... | collective-permute-start | bytes 884744 | tf_op jit(solution)/shard_map/ppermute | solution.py:312
  163.9 9.3 %collective-permute-start.27 = (bf16[192,768]{1,0:T(8,128)(2,1)S(1)}, bf16[192,768]{1,0:T(8,128)(2,1)S(1)}, u32[]{:S(2)}, u32[]{:S(2)}) collective-permute-start(bf16[192,768]{1,0:T(8,128)(2,1)S(1)} %add_convert_fusion), channel_id=1, source_target_pairs={{0,12},{4,0},{8,4},{12,8},{1,13},{5,1},{9,5},{13,9},{2,14},{6,2},{... | collective-permute-start | bytes 884744 | tf_op jit(solution)/shard_map/ppermute | solution.py:312
where the time goes:
time: 175 us; the launch traced here: 174 us
  waiting for transfers between devices  90.7 us (52%)
  Pallas kernels  38.7 us (22%)
  starting transfers between devices  35.8 us (20%)
  local copies, waits for them, and re-layouts  6.8 us (4%)
  other arithmetic  1.9 us (1%)
    ppermute x10, waiting for transfers between devices, tp_to(): return lax.ppermute(x, 'tp', perm)  60.2 us
    ppermute x5, waiting for transfers between devices, slab_to(): return lax.ppermute(x, 'slab', perm)  26.1 us
    pallas_call x2, Pallas kernels, qkv(): pl.pallas_call(functools.partial(qkv_kernel, bool(first)), out_shape=[jax...  23.5 us
    ppermute x5, starting transfers between devices, slab_to(): return lax.ppermute(x, 'slab', perm)  17.4 us
    pallas_call x2, Pallas kernels, attend(): pl.pallas_call(attend_kernel, out_shape=jax.ShapeDtypeStruct((ROWS, HF),...  11 us
    ppermute x10, starting transfers between devices, tp_to(): return lax.ppermute(x, 'tp', perm)  10.4 us
  transfers between devices with their start and end apart: 28, of which 17 were waited for; matrix products, arithmetic and copies ran while one was open for 3% of the time, Pallas kernels for 10%

commit v1 on v0

--- a/solution.py
+++ b/solution.py
@@ -45,32 +45,30 @@
 OUTER = other_side()
 
 
-def qkv_kernel(joined, meta, x0, xl, xr, xt, xb, wo, wc, wza, wzb, wca, wcb, scale_in, shift_in, qg_in, kg_in, *rest):
-    if joined:
-        first, q_ref, kv_ref, both_ref, wbuf, nbuf, xbuf, scale, shift, qg, kg, sems, wsems = rest
-    else:
-        q_ref, kv_ref, wbuf, nbuf, xbuf, scale, shift, qg, kg, sems, wsems = rest
-    far = pl.ds(HALF if joined else 0, HALF)
-    early = [(x0, xbuf.at[0]), (xl, xbuf.at[1]), (xr, xbuf.at[2]),
-             (xt.at[far], xbuf.at[3, pl.ds(0, HALF)]), (xb.at[far], xbuf.at[3, pl.ds(HALF, HALF)]),
+def qkv_kernel(meta, x0, xl, xr, xt, xb, wo, wc, wza, wzb, wca, wcb, scale_in, shift_in, qg_in, kg_in, *rest):
+    q_ref, kv_ref, wbuf, nbuf, xbuf, scale, shift, qg, kg, sems, wsems = rest
+    rows = pl.ds(0, ROWS)
+    early = [(x0.at[rows], xbuf.at[0]), (xl.at[rows], xbuf.at[1]), (xr.at[rows], xbuf.at[2]),
+             (xt, xbuf.at[3, pl.ds(0, HALF)]), (xb, xbuf.at[3, pl.ds(HALF, HALF)]),
              (scale_in, scale), (shift_in, shift), (qg_in, qg), (kg_in, kg)]
 
     def krows(k):
         return pl.ds(pl.multiple_of(meta[4 + k] * FS, FS), FS)
 
-    late = [(wo, wbuf.at[:, krows(0)]), (wc, wbuf.at[:, krows(1)]),
-            (wza, wbuf.at[0:1, krows(2)]), (wzb, wbuf.at[1:3, krows(2)]),
-            (wca, wbuf.at[0:1, krows(3)]), (wcb, wbuf.at[1:3, krows(3)])]
-    if joined:
-        late.append((first, both_ref.at[pl.ds(0, ROWS)]))
+    late = []
+    for k, parts in enumerate(((wo,), (wc,), (wza, wzb), (wca, wcb))):
+        blocks = [part.at[n] for part in parts for n in range(part.shape[0])]
+        late += [(block, wbuf.at[krows(k), pl.ds(p * HF, HF)]) for p, block in enumerate(blocks)]
     early = [pltpu.make_async_copy(src, dst, sems.at[n]) for n, (src, dst) in enumerate(early)]
     late = [pltpu.make_async_copy(src, dst, wsems.at[n]) for n, (src, dst) in enumerate(late)]
-    for copy in early + late:
+    for copy in early:
         copy.start()
     for copy in early:
         copy.wait()
-
-    step = 32
+    for copy in late:
+        copy.start()
+
+    step = 64
 
     def normalise(i, carry):
         r = pl.ds(pl.multiple_of(i * step, step), step)
@@ -89,33 +87,48 @@
     lax.fori_loop(0, ROWS // step, normalise, 0)
     for copy in late:
         copy.wait()
-    for p in (1, 2, 0):
-        acc = jnp.dot(nbuf[...], wbuf[p], preferred_element_type=F32)
-        if p == 2:
-            kv_ref[:, HF:] = acc.astype(BF16)
-            continue
-        gain = kg if p else qg
-        for h in range(HH):
-            part = acc[:, h * HD:(h + 1) * HD]
-            squares = jnp.mean(part * part, axis=-1, keepdims=True)
-            out = (part * lax.rsqrt(squares + 1e-06) * gain[...]).astype(BF16)
-            if p:
-                kv_ref[:, h * HD:(h + 1) * HD] = out
-            else:
-                q_ref[:, h * HD:(h + 1) * HD] = out
-        if p == 0 and joined:
-            both_ref[ROWS:, :] = kv_ref[...]
-
-
-def qkv(meta, xs, ws, scale, shift, qg, kg, *first):
-    shapes = [(ROWS, HF), (ROWS, 2 * HF)] + [(2 * ROWS, 2 * HF)] * len(first)
-    return pl.pallas_call(
-        functools.partial(qkv_kernel, bool(first)),
+    def head_norm(part, gain):
+        squares = jnp.mean(part * part, axis=-1, keepdims=True)
+        return (part * lax.rsqrt(squares + 1e-06) * gain[...]).astype(BF16)
+
+    acc = jnp.dot(nbuf[...], wbuf[...], preferred_element_type=F32)
+    for h in range(HH):
+        cols = slice(h * HD, (h + 1) * HD)
+        q_ref[:, cols] = head_norm(acc[:, cols], qg)
+        kv_ref[:, cols] = head_norm(acc[:, HF + h * HD:HF + (h + 1) * HD], kg)
+    kv_ref[:, HF:] = acc[:, 2 * HF:].astype(BF16)
+
+
+def join_kernel(first, second, crossed, out, sems):
+    copies = [pltpu.make_async_copy(src, out.at[pl.ds(n * ROWS, ROWS)], sems.at[n]) for n, src in enumerate((first, second))]
+    for copy in copies:
+        copy.start()
+    for copy in copies:
+        copy.wait()
+
+
+def join(first, second, crossed):
+    return pl.pallas_call(
+        join_kernel,
+        out_shape=jax.ShapeDtypeStruct((2 * ROWS, 2 * HF), BF16),
+        in_specs=[ANY] * 3,
+        out_specs=VM,
+        scratch_shapes=[pltpu.SemaphoreType.DMA((2,))],
+        compiler_params=pltpu.CompilerParams(vmem_limit_bytes=4 * 2**20),
+        cost_estimate=pl.CostEstimate(flops=10**11, bytes_accessed=4 * 2**20, transcendentals=0),
+        name="join",
+    )(first, second, crossed)
+
+
+def qkv(meta, xs, ws, scale, shift, qg, kg):
+    shapes = [(ROWS, HF), (ROWS, 2 * HF)]
+    return pl.pallas_call(
+        qkv_kernel,
         out_shape=[jax.ShapeDtypeStruct(shape, BF16) for shape in shapes],
-        in_specs=[SM] + [HBM] * (15 + len(first)),
+        in_specs=[SM] + [HBM] * 15,
         out_specs=[VM] * len(shapes),
         scratch_shapes=[
-            pltpu.VMEM((3, D, HF), BF16),
+            pltpu.VMEM((D, 3 * HF), BF16),
             pltpu.VMEM((ROWS, D), BF16),
             pltpu.VMEM((4, ROWS, FS), BF16),
             pltpu.VMEM((4, 1, FS), F32),
@@ -123,12 +136,12 @@
             pltpu.VMEM((1, HD), F32),
             pltpu.VMEM((1, HD), F32),
             pltpu.SemaphoreType.DMA((9,)),
-            pltpu.SemaphoreType.DMA((7,)),
+            pltpu.SemaphoreType.DMA((13,)),
         ],
         compiler_params=pltpu.CompilerParams(vmem_limit_bytes=56 * 2**20),
-        cost_estimate=pl.CostEstimate(flops=2 * ROWS * D * 3 * HF, bytes_accessed=10 * 2**20, transcendentals=0),
+        cost_estimate=pl.CostEstimate(flops=10**11, bytes_accessed=10 * 2**20, transcendentals=0),
         name="qkv",
-    )(meta, *xs, *ws, scale, shift, qg, kg, *first)
+    )(meta, *xs, *ws, scale, shift, qg, kg)
 
 
 def attend_kernel(meta, ids, q_ref, *rest):
@@ -314,34 +327,35 @@
     def slab_to(x, perm):
         return lax.ppermute(x, "slab", perm)
 
-    partner_tokens = pair(tokens)
     xl, xr = tp_to(tokens, RIGHT), tp_to(tokens, LEFT)
+    listed = jnp.concatenate([tile_ids, key_counts[:, None], key_counts[:, None]], axis=1)
+    below = jnp.pad(listed.astype(BF16), ((0, 13), (0, FS - WIN - 2)))
+    partner_all = pair(jnp.concatenate([tokens, below], axis=0))
+    partner_listed = partner_all[ROWS:ROWS + 3, :WIN + 2].astype(jnp.int32)
     w = w_qkv.transpose(1, 0, 2)
     w_own = lax.dynamic_slice_in_dim(w, side * HF, HF, 2)
     w_away = lax.dynamic_slice_in_dim(w, (1 - side) * HF, HF, 2)
     w_zb = lax.ppermute(w_away[1:], ("slab", "band"), OUTER)
-    w_za = pair(after(w_away[:1], partner_tokens))
+    w_za = pair(after(w_away[:1], partner_all))
     w_core = swap(w_own)
-    passed = after(partner_tokens, xl, xr)
+    xt, xb = tp_to(xl[:HALF], RIGHT), tp_to(xr[HALF:], LEFT)
+    passed = after(partner_all, xt, xb)
     pl_, pr_ = tp_to(passed, RIGHT), tp_to(passed, LEFT)
-    far_top = tp_to(jnp.concatenate([xl[:HALF], pl_[:HALF]], axis=0), RIGHT)
-    far_bottom = tp_to(jnp.concatenate([xr[HALF:], pr_[HALF:]], axis=0), LEFT)
-    own_x = (tokens, xl, xr, far_top, far_bottom)
-    partner_x = (partner_tokens, pl_, pr_, far_top, far_bottom)
-    w_za, w_zb = after(w_za, pl_, pr_), after(w_zb, pl_, pr_)
-    ws = [w_own, w_core, w_za, w_zb, swap(w_za), swap(w_zb)]
+    w_za, w_zb = after(w_za, xt, xb), after(w_zb, xt, xb)
+    ws = [after(w_own, pl_, pr_), w_core, w_za, w_zb, swap(w_za), swap(w_zb)]
 
     scale4, shift4 = scale.reshape(4, 1, FS), shift.reshape(4, 1, FS)
     qg, kg = q_gain.reshape(1, HD), k_gain.reshape(1, HD)
 
-    own_q, own_kv = qkv(meta, own_x, ws, scale4, shift4, qg, kg)
+    own_q, own_kv = qkv(meta, (tokens, xl, xr, xt, xb), ws, scale4, shift4, qg, kg)
     crossed = slab_to(own_kv, WRAP_Y)
-    partner_q, partner_kv, both = qkv(meta, partner_x, ws, scale4, shift4, qg, kg, own_kv)
-    listed = jnp.concatenate([tile_ids, key_counts[:, None], key_counts[:, None]], axis=1)
-    partner_listed = pair(after(listed, own_kv))
-    near = [both, slab_to(both, UP), slab_to(after(both, crossed), DOWN),
-            slab_to(after(crossed, partner_listed), WRAP_Z), slab_to(partner_kv, WRAP)]
-    pieces = near + [swap(x) for x in near]
+    pt, pb = tp_to(pl_[:HALF], RIGHT), tp_to(pr_[HALF:ROWS], LEFT)
+    partner_q, partner_kv = qkv(meta, (partner_all, pl_, pr_, pt, pb), ws, scale4, shift4, qg, kg)
+    second, direct = slab_to(crossed, WRAP_Z), slab_to(partner_kv, WRAP)
+    both = join(own_kv, partner_kv, crossed)
+    wrapped = [second, direct, swap(second), swap(direct)]
+    up, down = after(slab_to(both, UP), *wrapped), after(slab_to(both, DOWN), *wrapped)
+    pieces = [both, up, down, second, direct, swap(both), swap(up), swap(down)] + wrapped[2:]
     away = attend(meta, partner_listed, partner_q, pieces)
     back = pair(away)
     home = attend(meta, listed, after(own_q, away), pieces)

time: 175 us -> 172 us (0.983)
  the two profiles are of different devices: /device:TPU:166 before, /device:TPU:14 now
where the time goes in v1:
time: 172 us; the launch traced here: 171 us
  waiting for transfers between devices  82.8 us (48%)
  starting transfers between devices  38.7 us (23%)
  Pallas kernels  37.3 us (22%)
  local copies, waits for them, and re-layouts  9.93 us (6%)
  other arithmetic  1.99 us (1%)
    ppermute x12, waiting for transfers between devices, tp_to(): return lax.ppermute(x, 'tp', perm)  52.6 us
    ppermute x5, waiting for transfers between devices, slab_to(): return lax.ppermute(x, 'slab', perm)  20.6 us
    pallas_call x2, Pallas kernels, qkv(): pl.pallas_call(qkv_kernel, out_shape=[jax.ShapeDtypeStruct(shape, BF16) f...  19 us
    ppermute x5, starting transfers between devices, slab_to(): return lax.ppermute(x, 'slab', perm)  15.4 us
    ppermute x12, starting transfers between devices, tp_to(): return lax.ppermute(x, 'tp', perm)  13.9 us
    pallas_call x2, Pallas kernels, attend(): pl.pallas_call(attend_kernel, out_shape=jax.ShapeDtypeStruct((ROWS, HF),...  13.9 us
    ppermute x1, starting transfers between devices, shards(): w_zb = lax.ppermute(w_away[1:], ('slab', 'band'), OUTER)  5.86 us
  transfers between devices with their start and end apart: 29, of which 16 were waited for; matrix products, arithmetic and copies ran while one was open for 3% of the time, Pallas kernels for 15%

profile of v1, /device:TPU:14, one launch (start us, length us, event | category | flops | bytes accessed | tf_op | source)
XLA Modules:
  0.0 171.2 jit_solution(18146189033726503227)
XLA Ops:
  0.0 2.4 %dynamic-slice_bitcast_fusion = (bf16[3,768,384]{2,1,0:T(8,128)(2,1)S(1)}, bf16[3,768,384]{2,1,0:T(8,128)(2,1)S(1)}) fusion(bf16[768,3,768]{2,0,1:T(8,128)(2,1)} %param.11, s32[]{:T(128)S(6)} %select_n.40, s32[]{:T(128)S(6)} %select_n.39), kind=kLoop, calls=%fused_computation | loop fusion | bytes 7077896 | tf_op jit(solution)/shard_map/dynamic_slice | solution.py:337
  2.4 1.3 slice.39
  3.7 5.9 %collective-permute-start.9 = (bf16[2,768,384]{2,1,0:T(8,128)(2,1)}, bf16[2,768,384]{2,1,0:T(8,128)(2,1)}, u32[]{:S(2)}, u32[]{:S(2)}) collective-permute-start(bf16[2,768,384]{2,1,0:T(8,128)(2,1)} %slice.39), channel_id=1, source_target_pairs={{0,194},{1,195},{2,64},{3,65},{16,210},{17,211},{18,80},{19,81},{3... | collective-permute-start | bytes 3538952 | tf_op jit(solution)/shard_map/ppermute | solution.py:338
  9.5 0.5 collective-permute-start
  10.0 1.5 collective-permute-start.1
  11.6 0.1 copy.11
  11.7 0.1 fusion.2
  11.7 1.1 fusion.1
  12.8 0.1 collective-permute-start.4
  13.0 0.1 collective-permute-start.7
  13.1 11.6 %collective-permute-done.xl = bf16[384,768]{1,0:T(8,128)(2,1)} collective-permute-done((bf16[384,768]{1,0:T(8,128)(2,1)}, bf16[384,768]{1,0:T(8,128)(2,1)}, u32[]{:S(2)}, u32[]{:S(2)}) %collective-permute-start) | collective-permute-done | bytes 589856 | tf_op jit(solution)/shard_map/ppermute | solution.py:325
  24.6 1.0 slice.36
  25.6 1.8 %collective-permute-start.2 = (bf16[192,768]{1,0:T(8,128)(2,1)S(1)}, bf16[192,768]{1,0:T(8,128)(2,1)S(1)}, u32[]{:S(2)}, u32[]{:S(2)}) collective-permute-start(bf16[192,768]{1,0:T(8,128)(2,1)S(1)} %slice.36), channel_id=1, source_target_pairs={{0,4},{4,8},{8,12},{12,0},{1,5},{5,9},{9,13},{13,1},{2,6},{6,10},{... | collective-permute-start | bytes 884744 | tf_op jit(solution)/shard_map/ppermute | solution.py:325
  27.4 1.0 slice.37
  28.4 0.4 collective-permute-start.3
  28.8 0.1 slice.38
  28.9 0.1 collective-permute-start.8
  29.0 4.3 %collective-permute-done.2.xt = bf16[192,768]{1,0:T(8,128)(2,1)S(1)} collective-permute-done((bf16[192,768]{1,0:T(8,128)(2,1)S(1)}, bf16[192,768]{1,0:T(8,128)(2,1)S(1)}, u32[]{:S(2)}, u32[]{:S(2)}) %collective-permute-start.2) | collective-permute-done | bytes 294944 | tf_op jit(solution)/shard_map/ppermute | solution.py:325
  33.3 3.7 %collective-permute-done.3.xb = bf16[192,768]{1,0:T(8,128)(2,1)S(1)} collective-permute-done((bf16[192,768]{1,0:T(8,128)(2,1)S(1)}, bf16[192,768]{1,0:T(8,128)(2,1)S(1)}, u32[]{:S(2)}, u32[]{:S(2)}) %collective-permute-start.3) | collective-permute-done | bytes 294944 | tf_op jit(solution)/shard_map/ppermute | solution.py:325
  37.0 0.1 collective-permute-start.5
  37.0 2.0 %collective-permute-start.6 = (bf16[400,768]{1,0:T(8,128)(2,1)}, bf16[400,768]{1,0:T(8,128)(2,1)}, u32[]{:S(2)}, u32[]{:S(2)}) collective-permute-start(bf16[400,768]{1,0:T(8,128)(2,1)} %collective-permute-done.4.x0), channel_id=1, source_target_pairs={{0,12},{4,0},{8,4},{12,8},{1,13},{5,1},{9,5},{13,9},{2,14},{6,2},{... | collective-permute-start | bytes 1843208 | tf_op jit(solution)/shard_map/ppermute | solution.py:325
  39.1 3.3 %collective-permute-done.8.wza = bf16[1,768,384]{2,1,0:T(8,128)(2,1)} collective-permute-done((bf16[1,768,384]{2,1,0:T(8,128)(2,1)S(1)}, bf16[1,768,384]{2,1,0:T(8,128)(2,1)}, u32[]{:S(2)}, u32[]{:S(2)}) %collective-permute-start.8) | collective-permute-done | bytes 589856 | tf_op jit(solution)/shard_map/ppermute | solution.py:339
  42.4 0.6 stack.51.meta
  43.1 10.4 %collective-permute-done.5.xl = bf16[400,768]{1,0:T(8,128)(2,1)S(1)} collective-permute-done((bf16[400,768]{1,0:T(8,128)(2,1)}, bf16[400,768]{1,0:T(8,128)(2,1)S(1)}, u32[]{:S(2)}, u32[]{:S(2)}) %collective-permute-start.5) | collective-permute-done | bytes 614432 | tf_op jit(solution)/shard_map/ppermute | solution.py:325
  53.4 1.3 collective-permute-done.6.xr
  54.8 0.3 collective-permute-start.12
  55.0 1.0 slice.42
  56.0 2.1 %collective-permute-start.13 = (bf16[192,768]{1,0:T(8,128)(2,1)S(1)}, bf16[192,768]{1,0:T(8,128)(2,1)S(1)}, u32[]{:S(2)}, u32[]{:S(2)}) collective-permute-start(bf16[192,768]{1,0:T(8,128)(2,1)S(1)} %slice.42), channel_id=1, source_target_pairs={{0,12},{4,0},{8,4},{12,8},{1,13},{5,1},{9,5},{13,9},{2,14},{6,2},{... | collective-permute-start | bytes 884744 | tf_op jit(solution)/shard_map/ppermute | solution.py:325
  58.1 9.5 %qkv.2 = (bf16[384,384]{1,0:T(8,128)(2,1)}, bf16[384,768]{1,0:T(8,128)(2,1)}) custom-call(s32[12]{0:T(128)} %stack.51.meta, bf16[384,768]{1,0:T(8,128)(2,1)} %x0.1, bf16[384,768]{1,0:T(8,128)(2,1)} %collective-permute-done.xl, bf16[384,768]{1,0:T(8,128)(2,1)} %collective-permute-done.1.xr, bf16[192,768]{1,0:T(8,128)(2,1)} %copy-done.10, ...), custom_call_target="tpu_custom_call" | custom-call | flops 99999997952 | bytes 10485760 | tf_op jit(solution)/shard_map/qkv/pallas_call | solution.py:125
  67.7 0.8 collective-permute-start.14
  68.5 0.7 copy-done.12
  69.2 0.7 copy-done.13
  70.0 9.5 %qkv.3 = (bf16[384,384]{1,0:T(8,128)(2,1)}, bf16[384,768]{1,0:T(8,128)(2,1)}) custom-call(s32[12]{0:T(128)} %stack.51.meta, bf16[400,768]{1,0:T(8,128)(2,1)} %collective-permute-done.4.x0, bf16[400,768]{1,0:T(8,128)(2,1)} %copy-done.6, bf16[400,768]{1,0:T(8,128)(2,1)} %collective-permute-done.6.xr, bf16[192,768]{1,0:T(8,128)(2,1)} %copy-done.12, ...), custom_call_target="tpu_custom_call" | custom-call | flops 99999997952 | bytes 10485760 | tf_op jit(solution)/shard_map/qkv/pallas_call | solution.py:125
  79.5 0.8 collective-permute-start.17
  80.3 0.7 collective-permute-start.16
  81.0 1.1 copy-done.4
  82.1 0.3 join.1.rest_0_
  82.4 3.5 %collective-permute-start.15 = (bf16[768,768]{1,0:T(8,128)(2,1)S(1)}, bf16[768,768]{1,0:T(8,128)(2,1)S(1)}, u32[]{:S(2)}, u32[]{:S(2)}) collective-permute-start(bf16[768,768]{1,0:T(8,128)(2,1)S(1)} %join.1.rest_0_), channel_id=1, source_target_pairs={{0,16},{16,32},{32,48},{64,80},{80,96},{96,112},{128,144},{144,160... | collective-permute-start | bytes 3538952 | tf_op jit(solution)/shard_map/ppermute | solution.py:328
  85.8 9.5 %collective-permute-start.20 = (bf16[768,768]{1,0:T(8,128)(2,1)S(1)}, bf16[768,768]{1,0:T(8,128)(2,1)S(1)}, u32[]{:S(2)}, u32[]{:S(2)}) collective-permute-start(bf16[768,768]{1,0:T(8,128)(2,1)S(1)} %join.1.rest_0_), channel_id=1, source_target_pairs={{16,0},{32,16},{48,32},{80,64},{96,80},{112,96},{144,128},{160,144... | collective-permute-start | bytes 3538952 | tf_op jit(solution)/shard_map/ppermute | solution.py:328
  95.4 0.1 collective-permute-start.19
  95.5 0.5 collective-permute-start.18
  96.0 0.1 collective-permute-start.21
  96.1 1.4 collective-permute-done.19.rest_9_
  97.5 0.8 collective-permute-done.18.rest_8_
  98.3 19.3 %collective-permute-done.15.rest_1_ = bf16[768,768]{1,0:T(8,128)(2,1)S(1)} collective-permute-done((bf16[768,768]{1,0:T(8,128)(2,1)S(1)}, bf16[768,768]{1,0:T(8,128)(2,1)S(1)}, u32[]{:S(2)}, u32[]{:S(2)}) %collective-permute-start.15) | collective-permute-done | bytes 1179680 | tf_op jit(solution)/shard_map/ppermute | solution.py:328
  117.6 1.3 collective-permute-done.20.rest_2_
  118.9 0.5 collective-permute-start.23
  119.4 0.7 slice_convert_fusion.ids
  120.1 1.6 collective-permute-done.22.rest_6_
  121.7 1.7 collective-permute-done.23.rest_7_
  123.4 7.3 %attend.2 = bf16[384,384]{1,0:T(8,128)(2,1)S(1)} custom-call(s32[12]{0:T(128)S(1)} %copy-done.2, s32[3,16]{1,0:T(4,128)S(1)} %slice_convert_fusion.ids, bf16[384,384]{1,0:T(8,128)(2,1)S(1)} %copy-done.1, bf16[768,768]{1,0:T(8,128)(2,1)S(1)} %join.1.rest_0_, bf16[768,768]{1,0:T(8,128)(2,1)S(1)} %collective-permute-done.15.rest_1_, ...), custom_call_target="tpu_custom_call" | custom-call | flops 1056964608 | bytes 8388608 | tf_op jit(solution)/shard_map/attend/pallas_call | solution.py:227
  130.8 2.1 %collective-permute-start.24 = (bf16[384,384]{1,0:T(8,128)(2,1)S(1)}, bf16[384,384]{1,0:T(8,128)(2,1)S(1)}, u32[]{:S(2)}, u32[]{:S(2)}) collective-permute-start(bf16[384,384]{1,0:T(8,128)(2,1)S(1)} %attend.2), channel_id=1, source_target_pairs={{0,2},{1,3},{2,0},{3,1},{4,6},{5,7},{6,4},{7,5},{8,10},{9,11},{10,... | collective-permute-start | bytes 884744 | tf_op jit(solution)/shard_map/ppermute | solution.py:360
  132.9 6.6 %attend.3.home = bf16[384,384]{1,0:T(8,128)(2,1)S(1)} custom-call(s32[12]{0:T(128)S(1)} %copy-done.2, s32[3,16]{1,0:T(4,128)S(1)} %get-tuple-element.40.ids, bf16[384,384]{1,0:T(8,128)(2,1)S(1)} %copy-done, bf16[768,768]{1,0:T(8,128)(2,1)S(1)} %join.1.rest_0_, bf16[768,768]{1,0:T(8,128)(2,1)S(1)} %collective-permute-done.15.rest_1_, ...), custom_call_target="tpu_custom_call" | custom-call | flops 1056964608 | bytes 8388608 | tf_op jit(solution)/shard_map/attend/pallas_call | solution.py:227
  139.4 0.7 collective-permute-done.24.back
  140.2 3.2 %out_proj.1 = (bf16[384,768]{1,0:T(8,128)(2,1)S(1)}, bf16[384,768]{1,0:T(8,128)(2,1)S(1)}, f32[192,768]{1,0:T(8,128)S(1)}, f32[192,768]{1,0:T(8,128)S(1)}, f32[384,768]{1,0:T(8,128)S(1)}) custom-call(s32[12]{0:T(128)S(1)} %copy-done.2, bf16[384,384]{1,0:T(8,128)(2,1)S(1)} %attend.3.home, bf16[384,384]{1,0:T(8,128)(2,1)S(1)} %collective-permute-done.24.back, ...), custom_call_target="tpu_custom_call" | custom-call | flops 1811939328 | bytes 8388608 | tf_op jit(solution)/shard_map/out_proj/pallas_call | solution.py:265
  143.4 1.8 %collective-permute-start.25 = (bf16[384,768]{1,0:T(8,128)(2,1)S(1)}, bf16[384,768]{1,0:T(8,128)(2,1)S(1)}, u32[]{:S(2)}, u32[]{:S(2)}) collective-permute-start(bf16[384,768]{1,0:T(8,128)(2,1)S(1)} %get-tuple-element.35), channel_id=1, source_target_pairs={{0,4},{4,8},{8,12},{12,0},{1,5},{5,9},{9,13},{13,1},{2,6},{6,10},{... | collective-permute-start | bytes 1769480 | tf_op jit(solution)/shard_map/ppermute | solution.py:325
  145.2 0.3 collective-permute-start.26
  145.5 12.8 %collective-permute-done.25.from_left = bf16[384,768]{1,0:T(8,128)(2,1)S(1)} collective-permute-done((bf16[384,768]{1,0:T(8,128)(2,1)S(1)}, bf16[384,768]{1,0:T(8,128)(2,1)S(1)}, u32[]{:S(2)}, u32[]{:S(2)}) %collective-permute-start.25) | collective-permute-done | bytes 589856 | tf_op jit(solution)/shard_map/ppermute | solution.py:325
  158.4 3.0 %collective-permute-start.27 = (bf16[192,768]{1,0:T(8,128)(2,1)S(1)}, bf16[192,768]{1,0:T(8,128)(2,1)S(1)}, u32[]{:S(2)}, u32[]{:S(2)}) collective-permute-start(bf16[192,768]{1,0:T(8,128)(2,1)S(1)} %add_convert_fusion.1), channel_id=1, source_target_pairs={{0,4},{4,8},{8,12},{12,0},{1,5},{5,9},{9,13},{13,1},{2,6},{6,10},{... | collective-permute-start | bytes 884744 | tf_op jit(solution)/shard_map/ppermute | solution.py:325
  161.4 0.1 add_convert_fusion
  161.5 0.1 collective-permute-start.28
  161.6 5.0 %collective-permute-done.27.left_sum = bf16[192,768]{1,0:T(8,128)(2,1)S(1)} collective-permute-done((bf16[192,768]{1,0:T(8,128)(2,1)S(1)}, bf16[192,768]{1,0:T(8,128)(2,1)S(1)}, u32[]{:S(2)}, u32[]{:S(2)}) %collective-permute-start.27) | collective-permute-done | bytes 294944 | tf_op jit(solution)/shard_map/ppermute | solution.py:325
  166.5 3.6 %collective-permute-done.28.right_sum = bf16[192,768]{1,0:T(8,128)(2,1)S(1)} collective-permute-done((bf16[192,768]{1,0:T(8,128)(2,1)S(1)}, bf16[192,768]{1,0:T(8,128)(2,1)S(1)}, u32[]{:S(2)}, u32[]{:S(2)}) %collective-permute-start.28) | collective-permute-done | bytes 294944 | tf_op jit(solution)/shard_map/ppermute | solution.py:325
  170.1 1.1 last_sum.1
  (49 shorter events, 0.2 us)
Async XLA Ops:
  2.4 10.6 %copy-start.5 = (bf16[3,768,384]{2,1,0:T(8,128)(2,1)}, bf16[3,768,384]{2,1,0:T(8,128)(2,1)S(1)}, u32[]{:S(2)}) copy-start(bf16[3,768,384]{2,1,0:T(8,128)(2,1)S(1)} %get-tuple-element.23.wo) | copy-start | bytes 5308420
  2.4 9.2 %copy-start.9 = (s32[3]{0:T(128)S(1)}, s32[3]{0:T(128)}, u32[]{:S(2)}) copy-start(s32[3]{0:T(128)} %param.19) | copy-start | bytes 40
  2.4 9.3 %copy-start.8 = (s32[3,14]{1,0:T(4,128)S(1)}, s32[3,14]{1,0:T(4,128)}, u32[]{:S(2)}) copy-start(s32[3,14]{1,0:T(4,128)} %param.18) | copy-start | bytes 508
  3.7 33.3 %collective-permute-start.9 = (bf16[2,768,384]{2,1,0:T(8,128)(2,1)}, bf16[2,768,384]{2,1,0:T(8,128)(2,1)}, u32[]{:S(2)}, u32[]{:S(2)}) collective-permute-start(bf16[2,768,384]{2,1,0:T(8,128)(2,1)} %slice.39), channel_id=1, source_target_pairs={{0,194},{1,195},{2,64},{3,65},{16,210},{17,211},{18,80},{19,81},{3... | collective-permute-start | bytes 3538952 | tf_op jit(solution)/shard_map/ppermute | solution.py:338
  9.5 15.1 %collective-permute-start = (bf16[384,768]{1,0:T(8,128)(2,1)}, bf16[384,768]{1,0:T(8,128)(2,1)}, u32[]{:S(2)}, u32[]{:S(2)}) collective-permute-start(bf16[384,768]{1,0:T(8,128)(2,1)} %x0.1), channel_id=1, source_target_pairs={{0,4},{4,8},{8,12},{12,0},{1,5},{5,9},{9,13},{13,1},{2,6},{6,10},{... | collective-permute-start | bytes 1769480 | tf_op jit(solution)/shard_map/ppermute | solution.py:325
  10.0 17.4 %collective-permute-start.1 = (bf16[384,768]{1,0:T(8,128)(2,1)}, bf16[384,768]{1,0:T(8,128)(2,1)}, u32[]{:S(2)}, u32[]{:S(2)}) collective-permute-start(bf16[384,768]{1,0:T(8,128)(2,1)} %x0.1), channel_id=1, source_target_pairs={{0,12},{4,0},{8,4},{12,8},{1,13},{5,1},{9,5},{13,9},{2,14},{6,2},{... | collective-permute-start | bytes 1769480 | tf_op jit(solution)/shard_map/ppermute | solution.py:325
  12.8 16.0 %collective-permute-start.4 = (bf16[400,768]{1,0:T(8,128)(2,1)S(1)}, bf16[400,768]{1,0:T(8,128)(2,1)}, u32[]{:S(2)}, u32[]{:S(2)}) collective-permute-start(bf16[400,768]{1,0:T(8,128)(2,1)S(1)} %fusion.1), channel_id=1, source_target_pairs={{0,2},{1,3},{2,0},{3,1},{4,6},{5,7},{6,4},{7,5},{8,10},{9,11},{10,... | collective-permute-start | bytes 1843208 | tf_op jit(solution)/shard_map/ppermute | solution.py:333
  13.0 45.2 %collective-permute-start.7 = (bf16[3,768,384]{2,1,0:T(8,128)(2,1)S(1)}, bf16[3,768,384]{2,1,0:T(8,128)(2,1)}, u32[]{:S(2)}, u32[]{:S(2)}) collective-permute-start(bf16[3,768,384]{2,1,0:T(8,128)(2,1)S(1)} %get-tuple-element.23.wo), channel_id=1, source_target_pairs={{0,1},{1,0},{2,3},{3,2},{4,5},{5,4},{6,7},{7,6},{8,9},{9,8},{10,11... | collective-permute-start | bytes 5308424 | tf_op jit(solution)/shard_map/ppermute | solution.py:340
  25.6 7.6 %collective-permute-start.2 = (bf16[192,768]{1,0:T(8,128)(2,1)S(1)}, bf16[192,768]{1,0:T(8,128)(2,1)S(1)}, u32[]{:S(2)}, u32[]{:S(2)}) collective-permute-start(bf16[192,768]{1,0:T(8,128)(2,1)S(1)} %slice.36), channel_id=1, source_target_pairs={{0,4},{4,8},{8,12},{12,0},{1,5},{5,9},{9,13},{13,1},{2,6},{6,10},{... | collective-permute-start | bytes 884744 | tf_op jit(solution)/shard_map/ppermute | solution.py:325
  28.4 8.6 %collective-permute-start.3 = (bf16[192,768]{1,0:T(8,128)(2,1)S(1)}, bf16[192,768]{1,0:T(8,128)(2,1)S(1)}, u32[]{:S(2)}, u32[]{:S(2)}) collective-permute-start(bf16[192,768]{1,0:T(8,128)(2,1)S(1)} %slice.37), channel_id=1, source_target_pairs={{0,12},{4,0},{8,4},{12,8},{1,13},{5,1},{9,5},{13,9},{2,14},{6,2},{... | collective-permute-start | bytes 884744 | tf_op jit(solution)/shard_map/ppermute | solution.py:325
  28.9 13.5 %collective-permute-start.8 = (bf16[1,768,384]{2,1,0:T(8,128)(2,1)S(1)}, bf16[1,768,384]{2,1,0:T(8,128)(2,1)}, u32[]{:S(2)}, u32[]{:S(2)}) collective-permute-start(bf16[1,768,384]{2,1,0:T(8,128)(2,1)S(1)} %slice.38), channel_id=1, source_target_pairs={{0,2},{1,3},{2,0},{3,1},{4,6},{5,7},{6,4},{7,5},{8,10},{9,11},{10,... | collective-permute-start | bytes 1769480 | tf_op jit(solution)/shard_map/ppermute | solution.py:339
  33.3 9.1 %copy-start.10 = (bf16[192,768]{1,0:T(8,128)(2,1)}, bf16[192,768]{1,0:T(8,128)(2,1)S(1)}, u32[]{:S(2)}) copy-start(bf16[192,768]{1,0:T(8,128)(2,1)S(1)} %collective-permute-done.2.xt) | copy-start | bytes 884740
  36.9 5.4 %copy-start.11 = (bf16[192,768]{1,0:T(8,128)(2,1)}, bf16[192,768]{1,0:T(8,128)(2,1)S(1)}, u32[]{:S(2)}) copy-start(bf16[192,768]{1,0:T(8,128)(2,1)S(1)} %collective-permute-done.3.xb) | copy-start | bytes 884740
  36.9 21.2 %collective-permute-start.11 = (bf16[2,768,384]{2,1,0:T(8,128)(2,1)}, bf16[2,768,384]{2,1,0:T(8,128)(2,1)}, u32[]{:S(2)}, u32[]{:S(2)}) collective-permute-start(bf16[2,768,384]{2,1,0:T(8,128)(2,1)} %collective-permute-done.9.wzb), channel_id=1, source_target_pairs={{0,1},{1,0},{2,3},{3,2},{4,5},{5,4},{6,7},{7,6},{8,9},{9,8},{10,11... | collective-permute-start | bytes 3538952 | tf_op jit(solution)/shard_map/ppermute | solution.py:345
  37.0 16.5 %collective-permute-start.5 = (bf16[400,768]{1,0:T(8,128)(2,1)}, bf16[400,768]{1,0:T(8,128)(2,1)S(1)}, u32[]{:S(2)}, u32[]{:S(2)}) collective-permute-start(bf16[400,768]{1,0:T(8,128)(2,1)} %collective-permute-done.4.x0), channel_id=1, source_target_pairs={{0,4},{4,8},{8,12},{12,0},{1,5},{5,9},{9,13},{13,1},{2,6},{6,10},{... | collective-permute-start | bytes 1843208 | tf_op jit(solution)/shard_map/ppermute | solution.py:325
  37.0 17.7 %collective-permute-start.6 = (bf16[400,768]{1,0:T(8,128)(2,1)}, bf16[400,768]{1,0:T(8,128)(2,1)}, u32[]{:S(2)}, u32[]{:S(2)}) collective-permute-start(bf16[400,768]{1,0:T(8,128)(2,1)} %collective-permute-done.4.x0), channel_id=1, source_target_pairs={{0,12},{4,0},{8,4},{12,8},{1,13},{5,1},{9,5},{13,9},{2,14},{6,2},{... | collective-permute-start | bytes 1843208 | tf_op jit(solution)/shard_map/ppermute | solution.py:325
  42.4 15.7 %collective-permute-start.10 = (bf16[1,768,384]{2,1,0:T(8,128)(2,1)}, bf16[1,768,384]{2,1,0:T(8,128)(2,1)}, u32[]{:S(2)}, u32[]{:S(2)}) collective-permute-start(bf16[1,768,384]{2,1,0:T(8,128)(2,1)} %collective-permute-done.8.wza), channel_id=1, source_target_pairs={{0,1},{1,0},{2,3},{3,2},{4,5},{5,4},{6,7},{7,6},{8,9},{9,8},{10,11... | collective-permute-start | bytes 1769480 | tf_op jit(solution)/shard_map/ppermute | solution.py:345
  53.4 14.2 %copy-start.6 = (bf16[400,768]{1,0:T(8,128)(2,1)}, bf16[400,768]{1,0:T(8,128)(2,1)S(1)}, u32[]{:S(2)}) copy-start(bf16[400,768]{1,0:T(8,128)(2,1)S(1)} %collective-permute-done.5.xl) | copy-start | bytes 1843204
  54.8 13.7 %collective-permute-start.12 = (bf16[192,768]{1,0:T(8,128)(2,1)S(1)}, bf16[192,768]{1,0:T(8,128)(2,1)S(1)}, u32[]{:S(2)}, u32[]{:S(2)}) collective-permute-start(bf16[192,768]{1,0:T(8,128)(2,1)S(1)} %slice.41), channel_id=1, source_target_pairs={{0,4},{4,8},{8,12},{12,0},{1,5},{5,9},{9,13},{13,1},{2,6},{6,10},{... | collective-permute-start | bytes 884744 | tf_op jit(solution)/shard_map/ppermute | solution.py:325
  56.0 12.5 %collective-permute-start.13 = (bf16[192,768]{1,0:T(8,128)(2,1)S(1)}, bf16[192,768]{1,0:T(8,128)(2,1)S(1)}, u32[]{:S(2)}, u32[]{:S(2)}) collective-permute-start(bf16[192,768]{1,0:T(8,128)(2,1)S(1)} %slice.42), channel_id=1, source_target_pairs={{0,12},{4,0},{8,4},{12,8},{1,13},{5,1},{9,5},{13,9},{2,14},{6,2},{... | collective-permute-start | bytes 884744 | tf_op jit(solution)/shard_map/ppermute | solution.py:325
  67.6 13.4 %copy-start.3 = (bf16[384,768]{1,0:T(8,128)(2,1)S(1)}, bf16[384,768]{1,0:T(8,128)(2,1)}, u32[]{:S(2)}) copy-start(bf16[384,768]{1,0:T(8,128)(2,1)} %get-tuple-element.29.first) | copy-start | bytes 1769476
  67.7 12.6 %collective-permute-start.14 = (bf16[384,768]{1,0:T(8,128)(2,1)}, bf16[384,768]{1,0:T(8,128)(2,1)S(1)}, u32[]{:S(2)}, u32[]{:S(2)}) collective-permute-start(bf16[384,768]{1,0:T(8,128)(2,1)} %get-tuple-element.29.first), channel_id=1, source_target_pairs={{48,0},{112,64},{176,128},{64,112},{128,176},{192,240},{49,1},{113... | collective-permute-start | bytes 1769480 | tf_op jit(solution)/shard_map/ppermute | solution.py:328
  68.5 0.7 copy-start.12
  69.2 0.7 copy-start.13
  79.4 44.0 %copy-start.1 = (bf16[384,384]{1,0:T(8,128)(2,1)S(1)}, bf16[384,384]{1,0:T(8,128)(2,1)}, u32[]{:S(2)}) copy-start(bf16[384,384]{1,0:T(8,128)(2,1)} %get-tuple-element.28.q_ref) | copy-start | bytes 884740
  79.4 44.0 %copy-start.2 = (s32[12]{0:T(128)S(1)}, s32[12]{0:T(128)}, u32[]{:S(2)}) copy-start(s32[12]{0:T(128)} %stack.51.meta) | copy-start | bytes 148
  79.5 15.9 %collective-permute-start.17 = (bf16[384,768]{1,0:T(8,128)(2,1)}, bf16[384,768]{1,0:T(8,128)(2,1)S(1)}, u32[]{:S(2)}, u32[]{:S(2)}) collective-permute-start(bf16[384,768]{1,0:T(8,128)(2,1)} %get-tuple-element.30.second), channel_id=1, source_target_pairs={{48,64},{112,128},{176,192},{64,48},{128,112},{192,176},{49,65},{1... | collective-permute-start | bytes 1769480 | tf_op jit(solution)/shard_map/ppermute | solution.py:328
  80.3 15.2 %collective-permute-start.16 = (bf16[384,768]{1,0:T(8,128)(2,1)S(1)}, bf16[384,768]{1,0:T(8,128)(2,1)S(1)}, u32[]{:S(2)}, u32[]{:S(2)}) collective-permute-start(bf16[384,768]{1,0:T(8,128)(2,1)S(1)} %collective-permute-done.14.crossed), channel_id=1, source_target_pairs={{0,64},{64,128},{128,192},{112,48},{176,112},{240,176},{1,65},{65,... | collective-permute-start | bytes 1769480 | tf_op jit(solution)/shard_map/ppermute | solution.py:328
  81.0 1.1 copy-start.4
  82.4 35.3 %collective-permute-start.15 = (bf16[768,768]{1,0:T(8,128)(2,1)S(1)}, bf16[768,768]{1,0:T(8,128)(2,1)S(1)}, u32[]{:S(2)}, u32[]{:S(2)}) collective-permute-start(bf16[768,768]{1,0:T(8,128)(2,1)S(1)} %join.1.rest_0_), channel_id=1, source_target_pairs={{0,16},{16,32},{32,48},{64,80},{80,96},{96,112},{128,144},{144,160... | collective-permute-start | bytes 3538952 | tf_op jit(solution)/shard_map/ppermute | solution.py:328
  85.8 33.0 %collective-permute-start.20 = (bf16[768,768]{1,0:T(8,128)(2,1)S(1)}, bf16[768,768]{1,0:T(8,128)(2,1)S(1)}, u32[]{:S(2)}, u32[]{:S(2)}) collective-permute-start(bf16[768,768]{1,0:T(8,128)(2,1)S(1)} %join.1.rest_0_), channel_id=1, source_target_pairs={{16,0},{32,16},{48,32},{80,64},{96,80},{112,96},{144,128},{160,144... | collective-permute-start | bytes 3538952 | tf_op jit(solution)/shard_map/ppermute | solution.py:328
  95.4 2.1 %collective-permute-start.19 = (bf16[384,768]{1,0:T(8,128)(2,1)S(1)}, bf16[384,768]{1,0:T(8,128)(2,1)S(1)}, u32[]{:S(2)}, u32[]{:S(2)}) collective-permute-start(bf16[384,768]{1,0:T(8,128)(2,1)S(1)} %collective-permute-done.17.rest_4_), channel_id=1, source_target_pairs={{0,1},{1,0},{2,3},{3,2},{4,5},{5,4},{6,7},{7,6},{8,9},{9,8},{10,11... | collective-permute-start | bytes 1769480 | tf_op jit(solution)/shard_map/ppermute | solution.py:356
  95.5 2.8 %collective-permute-start.18 = (bf16[384,768]{1,0:T(8,128)(2,1)S(1)}, bf16[384,768]{1,0:T(8,128)(2,1)S(1)}, u32[]{:S(2)}, u32[]{:S(2)}) collective-permute-start(bf16[384,768]{1,0:T(8,128)(2,1)S(1)} %collective-permute-done.16.rest_3_), channel_id=1, source_target_pairs={{0,1},{1,0},{2,3},{3,2},{4,5},{5,4},{6,7},{7,6},{8,9},{9,8},{10,11... | collective-permute-start | bytes 1769480 | tf_op jit(solution)/shard_map/ppermute | solution.py:356
  96.0 24.1 %collective-permute-start.21 = (bf16[768,768]{1,0:T(8,128)(2,1)S(1)}, bf16[768,768]{1,0:T(8,128)(2,1)S(1)}, u32[]{:S(2)}, u32[]{:S(2)}) collective-permute-start(bf16[768,768]{1,0:T(8,128)(2,1)S(1)} %join.1.rest_0_), channel_id=1, source_target_pairs={{0,1},{1,0},{2,3},{3,2},{4,5},{5,4},{6,7},{7,6},{8,9},{9,8},{10,11... | collective-permute-start | bytes 3538952 | tf_op jit(solution)/shard_map/ppermute | solution.py:358
  118.9 2.8 %collective-permute-start.22 = (bf16[768,768]{1,0:T(8,128)(2,1)S(1)}, bf16[768,768]{1,0:T(8,128)(2,1)S(1)}, u32[]{:S(2)}, u32[]{:S(2)}) collective-permute-start(bf16[768,768]{1,0:T(8,128)(2,1)S(1)} %collective-permute-done.15.rest_1_), channel_id=1, source_target_pairs={{0,1},{1,0},{2,3},{3,2},{4,5},{5,4},{6,7},{7,6},{8,9},{9,8},{10,11... | collective-permute-start | bytes 3538952 | tf_op jit(solution)/shard_map/ppermute | solution.py:358
  118.9 4.5 %collective-permute-start.23 = (bf16[768,768]{1,0:T(8,128)(2,1)S(1)}, bf16[768,768]{1,0:T(8,128)(2,1)S(1)}, u32[]{:S(2)}, u32[]{:S(2)}) collective-permute-start(bf16[768,768]{1,0:T(8,128)(2,1)S(1)} %collective-permute-done.20.rest_2_), channel_id=1, source_target_pairs={{0,1},{1,0},{2,3},{3,2},{4,5},{5,4},{6,7},{7,6},{8,9},{9,8},{10,11... | collective-permute-start | bytes 3538952 | tf_op jit(solution)/shard_map/ppermute | solution.py:358
  123.4 9.4 %copy-start = (bf16[384,384]{1,0:T(8,128)(2,1)S(1)}, bf16[384,384]{1,0:T(8,128)(2,1)}, u32[]{:S(2)}) copy-start(bf16[384,384]{1,0:T(8,128)(2,1)} %get-tuple-element.33.q_ref) | copy-start | bytes 884740
  123.4 16.7 %slice-start = ((s8[4718592]{0:T(1024)(128)(4,1)}), s8[4194304]{0:T(1024)(128)(4,1)S(1)}, s32[]{:S(2)}) async-start(s8[4718592]{0:T(1024)(128)(4,1)} %bitcast.21), calls=%async_computation | async-start | bytes 8388608
  130.8 9.4 %collective-permute-start.24 = (bf16[384,384]{1,0:T(8,128)(2,1)S(1)}, bf16[384,384]{1,0:T(8,128)(2,1)S(1)}, u32[]{:S(2)}, u32[]{:S(2)}) collective-permute-start(bf16[384,384]{1,0:T(8,128)(2,1)S(1)} %attend.2), channel_id=1, source_target_pairs={{0,2},{1,3},{2,0},{3,1},{4,6},{5,7},{6,4},{7,5},{8,10},{9,11},{10,... | collective-permute-start | bytes 884744 | tf_op jit(solution)/shard_map/ppermute | solution.py:360
  132.9 7.3 %slice-start.1 = ((s8[4718592]{0:T(1024)(128)(4,1)}), s8[524288]{0:T(1024)(128)(4,1)S(1)}, s32[]{:S(2)}) async-start(s8[4718592]{0:T(1024)(128)(4,1)} %bitcast.21), calls=%async_computation.1 | async-start | bytes 1048576
  143.4 18.2 %copy-start.7 = (f32[768]{0:T(1024)S(1)}, f32[768]{0:T(1024)}, u32[]{:S(2)}) copy-start(f32[768]{0:T(1024)} %param.15) | copy-start | bytes 9220
  143.4 14.9 %collective-permute-start.25 = (bf16[384,768]{1,0:T(8,128)(2,1)S(1)}, bf16[384,768]{1,0:T(8,128)(2,1)S(1)}, u32[]{:S(2)}, u32[]{:S(2)}) collective-permute-start(bf16[384,768]{1,0:T(8,128)(2,1)S(1)} %get-tuple-element.35), channel_id=1, source_target_pairs={{0,4},{4,8},{8,12},{12,0},{1,5},{5,9},{9,13},{13,1},{2,6},{6,10},{... | collective-permute-start | bytes 1769480 | tf_op jit(solution)/shard_map/ppermute | solution.py:325
  145.2 16.2 %collective-permute-start.26 = (bf16[384,768]{1,0:T(8,128)(2,1)S(1)}, bf16[384,768]{1,0:T(8,128)(2,1)S(1)}, u32[]{:S(2)}, u32[]{:S(2)}) collective-permute-start(bf16[384,768]{1,0:T(8,128)(2,1)S(1)} %get-tuple-element.36), channel_id=1, source_target_pairs={{0,12},{4,0},{8,4},{12,8},{1,13},{5,1},{9,5},{13,9},{2,14},{6,2},{... | collective-permute-start | bytes 1769480 | tf_op jit(solution)/shard_map/ppermute | solution.py:325
  158.4 8.2 %collective-permute-start.27 = (bf16[192,768]{1,0:T(8,128)(2,1)S(1)}, bf16[192,768]{1,0:T(8,128)(2,1)S(1)}, u32[]{:S(2)}, u32[]{:S(2)}) collective-permute-start(bf16[192,768]{1,0:T(8,128)(2,1)S(1)} %add_convert_fusion.1), channel_id=1, source_target_pairs={{0,4},{4,8},{8,12},{12,0},{1,5},{5,9},{9,13},{13,1},{2,6},{6,10},{... | collective-permute-start | bytes 884744 | tf_op jit(solution)/shard_map/ppermute | solution.py:325
  161.5 8.6 %collective-permute-start.28 = (bf16[192,768]{1,0:T(8,128)(2,1)S(1)}, bf16[192,768]{1,0:T(8,128)(2,1)S(1)}, u32[]{:S(2)}, u32[]{:S(2)}) collective-permute-start(bf16[192,768]{1,0:T(8,128)(2,1)S(1)} %add_convert_fusion), channel_id=1, source_target_pairs={{0,12},{4,0},{8,4},{12,8},{1,13},{5,1},{9,5},{13,9},{2,14},{6,2},{... | collective-permute-start | bytes 884744 | tf_op jit(solution)/shard_map/ppermute | solution.py:325

commit v2 on v1

--- a/solution.py
+++ b/solution.py
@@ -334,9 +334,9 @@
     partner_listed = partner_all[ROWS:ROWS + 3, :WIN + 2].astype(jnp.int32)
     w = w_qkv.transpose(1, 0, 2)
     w_own = lax.dynamic_slice_in_dim(w, side * HF, HF, 2)
-    w_away = lax.dynamic_slice_in_dim(w, (1 - side) * HF, HF, 2)
-    w_zb = lax.ppermute(w_away[1:], ("slab", "band"), OUTER)
-    w_za = pair(after(w_away[:1], partner_all))
+    away = (1 - side) * HF
+    w_zb = lax.ppermute(lax.dynamic_slice(w, (1, 0, away), (2, FS, HF)), ("slab", "band"), OUTER)
+    w_za = pair(after(lax.dynamic_slice(w, (0, 0, away), (1, FS, HF)), partner_all, partner_listed))
     w_core = swap(w_own)
     xt, xb = tp_to(xl[:HALF], RIGHT), tp_to(xr[HALF:], LEFT)
     passed = after(partner_all, xt, xb)

time: 172 us -> 173 us (level)
  Pallas kernels: 37.3 us -> 35 us
  local copies, waits for them, and re-layouts: 9.93 us -> 11.8 us
    ppermute x12, waiting for transfers between devices: 52.6 us -> 49.3 us  [tp_to(): return lax.ppermute(x, 'tp', perm)]
    pallas_call x2, Pallas kernels: 13.9 us -> 11.6 us  [attend(): pl.pallas_call(attend_kernel, out_shape=jax.ShapeDtypeStruct((ROWS, HF),...]
    unnamed x32 -> x30, local copies, waits for them, and re-layouts: 2.55 us -> 4.5 us
    ppermute x1, waiting for transfers between devices: 0.73 us -> 2.65 us  [shards(): back = pair(away)]
  transfers between devices with their start and end apart: 29 -> 29, of which waited for: 16 -> 16; matrix products, arithmetic and copies ran while one was open for 3% -> 5% of each run, Pallas kernels for 15% -> 14%
where the time goes in v2:
time: 173 us; the launch traced here: 171 us
  waiting for transfers between devices  82.7 us (48%)
  starting transfers between devices  38.1 us (22%)
  Pallas kernels  35 us (20%)
  local copies, waits for them, and re-layouts  11.8 us (7%)
  other arithmetic  2.77 us (2%)
    ppermute x12, waiting for transfers between devices, tp_to(): return lax.ppermute(x, 'tp', perm)  49.3 us
    ppermute x5, waiting for transfers between devices, slab_to(): return lax.ppermute(x, 'slab', perm)  20.6 us
    pallas_call x2, Pallas kernels, qkv(): pl.pallas_call(qkv_kernel, out_shape=[jax.ShapeDtypeStruct(shape, BF16) f...  19 us
    ppermute x5, starting transfers between devices, slab_to(): return lax.ppermute(x, 'slab', perm)  15.4 us
    ppermute x12, starting transfers between devices, tp_to(): return lax.ppermute(x, 'tp', perm)  13.9 us
    pallas_call x2, Pallas kernels, attend(): pl.pallas_call(attend_kernel, out_shape=jax.ShapeDtypeStruct((ROWS, HF),...  11.6 us
    ppermute x1, starting transfers between devices, shards(): lax.ppermute(lax.dynamic_slice(w, (1, 0, away), (2, FS, HF)), ('slab', 'b...  5.86 us
    unnamed x30, local copies, waits for them, and re-layouts  4.5 us
  transfers between devices with their start and end apart: 29, of which 16 were waited for; matrix products, arithmetic and copies ran while one was open for 5% of the time, Pallas kernels for 14%

profile of v2, /device:TPU:14, one launch (start us, length us, event | category | flops | bytes accessed | tf_op | source)
XLA Modules:
  0.0 170.8 jit_solution(15076494680584101133)
XLA Ops:
  0.0 2.0 %copy-done = bf16[768,3,768]{2,0,1:T(8,128)(2,1)S(1)} copy-done((bf16[768,3,768]{2,0,1:T(8,128)(2,1)S(1)}, bf16[768,3,768]{2,0,1:T(8,128)(2,1)}, u32[]{:S(2)}) %copy-start) | copy-done | bytes 3538968
  2.0 1.2 dynamic-slice_bitcast_fusion.1
  3.2 5.9 %collective-permute-start.9 = (bf16[2,768,384]{2,1,0:T(8,128)(2,1)}, bf16[2,768,384]{2,1,0:T(8,128)(2,1)}, u32[]{:S(2)}, u32[]{:S(2)}) collective-permute-start(bf16[2,768,384]{2,1,0:T(8,128)(2,1)} %dynamic-slice_bitcast_fusion.1), channel_id=1, source_target_pairs={{0,194},{1,195},{2,64},{3,65},{16,210},{17,211},{18,80},{19,81},{3... | collective-permute-start | bytes 3538952 | tf_op jit(solution)/shard_map/ppermute | solution.py:338
  9.0 0.5 collective-permute-start
  9.5 1.5 collective-permute-start.1
  11.1 0.1 copy.11
  11.2 0.1 fusion.2
  11.2 1.9 %fusion.1 = bf16[400,768]{1,0:T(8,128)(2,1)} fusion(bf16[3,16]{1,0:T(4,128)(2,1)S(1)} %get-tuple-element.39, bf16[384,768]{1,0:T(8,128)(2,1)} %x0.1), kind=kLoop, calls=%fused_computation.4 | loop fusion | flops 1843200 | bytes 1204320 | tf_op jit(solution)/shard_map/concatenate | solution.py:333
  13.1 1.4 dynamic-slice_bitcast_fusion.wo
  14.6 9.6 %collective-permute-done.xl = bf16[384,768]{1,0:T(8,128)(2,1)} collective-permute-done((bf16[384,768]{1,0:T(8,128)(2,1)}, bf16[384,768]{1,0:T(8,128)(2,1)}, u32[]{:S(2)}, u32[]{:S(2)}) %collective-permute-start) | collective-permute-done | bytes 589856 | tf_op jit(solution)/shard_map/ppermute | solution.py:325
  24.1 1.0 slice.28
  25.1 1.8 %collective-permute-start.2 = (bf16[192,768]{1,0:T(8,128)(2,1)S(1)}, bf16[192,768]{1,0:T(8,128)(2,1)S(1)}, u32[]{:S(2)}, u32[]{:S(2)}) collective-permute-start(bf16[192,768]{1,0:T(8,128)(2,1)S(1)} %slice.28), channel_id=1, source_target_pairs={{0,4},{4,8},{8,12},{12,0},{1,5},{5,9},{9,13},{13,1},{2,6},{6,10},{... | collective-permute-start | bytes 884744 | tf_op jit(solution)/shard_map/ppermute | solution.py:325
  26.9 1.0 slice.29
  27.9 0.4 collective-permute-start.3
  28.3 0.1 dynamic-slice_bitcast_fusion.2
  28.4 0.7 slice_convert_fusion.ids
  29.0 0.1 collective-permute-start.8
  29.2 3.6 %collective-permute-done.2.xt = bf16[192,768]{1,0:T(8,128)(2,1)S(1)} collective-permute-done((bf16[192,768]{1,0:T(8,128)(2,1)S(1)}, bf16[192,768]{1,0:T(8,128)(2,1)S(1)}, u32[]{:S(2)}, u32[]{:S(2)}) %collective-permute-start.2) | collective-permute-done | bytes 294944 | tf_op jit(solution)/shard_map/ppermute | solution.py:325
  32.8 3.7 %collective-permute-done.3.xb = bf16[192,768]{1,0:T(8,128)(2,1)S(1)} collective-permute-done((bf16[192,768]{1,0:T(8,128)(2,1)S(1)}, bf16[192,768]{1,0:T(8,128)(2,1)S(1)}, u32[]{:S(2)}, u32[]{:S(2)}) %collective-permute-start.3) | collective-permute-done | bytes 294944 | tf_op jit(solution)/shard_map/ppermute | solution.py:325
  36.5 0.1 collective-permute-start.5
  36.5 2.0 %collective-permute-start.6 = (bf16[400,768]{1,0:T(8,128)(2,1)}, bf16[400,768]{1,0:T(8,128)(2,1)}, u32[]{:S(2)}, u32[]{:S(2)}) collective-permute-start(bf16[400,768]{1,0:T(8,128)(2,1)} %collective-permute-done.4.x0), channel_id=1, source_target_pairs={{0,12},{4,0},{8,4},{12,8},{1,13},{5,1},{9,5},{13,9},{2,14},{6,2},{... | collective-permute-start | bytes 1843208 | tf_op jit(solution)/shard_map/ppermute | solution.py:325
  38.6 3.9 %collective-permute-done.8.wza = bf16[1,768,384]{2,1,0:T(8,128)(2,1)} collective-permute-done((bf16[1,768,384]{2,1,0:T(8,128)(2,1)S(1)}, bf16[1,768,384]{2,1,0:T(8,128)(2,1)}, u32[]{:S(2)}, u32[]{:S(2)}) %collective-permute-start.8) | collective-permute-done | bytes 589856 | tf_op jit(solution)/shard_map/ppermute | solution.py:339
  42.5 0.6 stack.51.meta
  43.1 9.9 %collective-permute-done.5.xl = bf16[400,768]{1,0:T(8,128)(2,1)} collective-permute-done((bf16[400,768]{1,0:T(8,128)(2,1)}, bf16[400,768]{1,0:T(8,128)(2,1)}, u32[]{:S(2)}, u32[]{:S(2)}) %collective-permute-start.5) | collective-permute-done | bytes 614432 | tf_op jit(solution)/shard_map/ppermute | solution.py:325
  53.0 1.2 collective-permute-done.6.xr
  54.2 1.0 slice.31
  55.2 0.4 collective-permute-start.12
  55.6 1.0 slice.32
  56.6 2.0 %collective-permute-start.13 = (bf16[192,768]{1,0:T(8,128)(2,1)S(1)}, bf16[192,768]{1,0:T(8,128)(2,1)S(1)}, u32[]{:S(2)}, u32[]{:S(2)}) collective-permute-start(bf16[192,768]{1,0:T(8,128)(2,1)S(1)} %slice.32), channel_id=1, source_target_pairs={{0,12},{4,0},{8,4},{12,8},{1,13},{5,1},{9,5},{13,9},{2,14},{6,2},{... | collective-permute-start | bytes 884744 | tf_op jit(solution)/shard_map/ppermute | solution.py:325
  58.6 9.5 %qkv.2 = (bf16[384,384]{1,0:T(8,128)(2,1)}, bf16[384,768]{1,0:T(8,128)(2,1)}) custom-call(s32[12]{0:T(128)} %stack.51.meta, bf16[384,768]{1,0:T(8,128)(2,1)} %x0.1, bf16[384,768]{1,0:T(8,128)(2,1)} %collective-permute-done.xl, bf16[384,768]{1,0:T(8,128)(2,1)} %collective-permute-done.1.xr, bf16[192,768]{1,0:T(8,128)(2,1)} %copy-done.9, ...), custom_call_target="tpu_custom_call" | custom-call | flops 99999997952 | bytes 10485760 | tf_op jit(solution)/shard_map/qkv/pallas_call | solution.py:125
  68.1 0.8 collective-permute-start.14
  69.0 0.7 copy-done.11
  69.7 0.7 copy-done.12
  70.4 9.5 %qkv.3 = (bf16[384,384]{1,0:T(8,128)(2,1)}, bf16[384,768]{1,0:T(8,128)(2,1)}) custom-call(s32[12]{0:T(128)} %stack.51.meta, bf16[400,768]{1,0:T(8,128)(2,1)} %collective-permute-done.4.x0, bf16[400,768]{1,0:T(8,128)(2,1)} %collective-permute-done.5.xl, bf16[400,768]{1,0:T(8,128)(2,1)} %collective-permute-done.6.xr, bf16[192,768]{1,0:T(8,128)(2,1)} %copy-done.11, ...), custom_call_target="tpu_custom_call" | custom-call | flops 99999997952 | bytes 10485760 | tf_op jit(solution)/shard_map/qkv/pallas_call | solution.py:125
  79.9 0.8 collective-permute-start.17
  80.7 0.7 collective-permute-start.16
  81.5 1.1 copy-done.5
  82.5 0.3 join.1.rest_0_
  82.8 3.5 %collective-permute-start.15 = (bf16[768,768]{1,0:T(8,128)(2,1)S(1)}, bf16[768,768]{1,0:T(8,128)(2,1)S(1)}, u32[]{:S(2)}, u32[]{:S(2)}) collective-permute-start(bf16[768,768]{1,0:T(8,128)(2,1)S(1)} %join.1.rest_0_), channel_id=1, source_target_pairs={{0,16},{16,32},{32,48},{64,80},{80,96},{96,112},{128,144},{144,160... | collective-permute-start | bytes 3538952 | tf_op jit(solution)/shard_map/ppermute | solution.py:328
  86.3 9.5 %collective-permute-start.20 = (bf16[768,768]{1,0:T(8,128)(2,1)S(1)}, bf16[768,768]{1,0:T(8,128)(2,1)S(1)}, u32[]{:S(2)}, u32[]{:S(2)}) collective-permute-start(bf16[768,768]{1,0:T(8,128)(2,1)S(1)} %join.1.rest_0_), channel_id=1, source_target_pairs={{16,0},{32,16},{48,32},{80,64},{96,80},{112,96},{144,128},{160,144... | collective-permute-start | bytes 3538952 | tf_op jit(solution)/shard_map/ppermute | solution.py:328
  95.8 0.1 collective-permute-start.19
  95.9 0.5 collective-permute-start.18
  96.4 0.1 collective-permute-start.21
  96.5 1.4 collective-permute-done.19.rest_9_
  97.9 0.8 collective-permute-done.18.rest_8_
  98.8 19.3 %collective-permute-done.15.rest_1_ = bf16[768,768]{1,0:T(8,128)(2,1)S(1)} collective-permute-done((bf16[768,768]{1,0:T(8,128)(2,1)S(1)}, bf16[768,768]{1,0:T(8,128)(2,1)S(1)}, u32[]{:S(2)}, u32[]{:S(2)}) %collective-permute-start.15) | collective-permute-done | bytes 1179680 | tf_op jit(solution)/shard_map/ppermute | solution.py:328
  118.1 1.3 collective-permute-done.20.rest_2_
  119.3 0.5 collective-permute-start.23
  119.8 2.3 %collective-permute-done.22.rest_6_ = bf16[768,768]{1,0:T(8,128)(2,1)S(1)} collective-permute-done((bf16[768,768]{1,0:T(8,128)(2,1)S(1)}, bf16[768,768]{1,0:T(8,128)(2,1)S(1)}, u32[]{:S(2)}, u32[]{:S(2)}) %collective-permute-start.22) | collective-permute-done | bytes 1179680 | tf_op jit(solution)/shard_map/ppermute | solution.py:358
  122.2 1.7 collective-permute-done.23.rest_7_
  123.9 6.4 %attend.2 = bf16[384,384]{1,0:T(8,128)(2,1)S(1)} custom-call(s32[12]{0:T(128)S(1)} %copy-done.3, s32[3,16]{1,0:T(4,128)S(1)} %slice_convert_fusion.ids, bf16[384,384]{1,0:T(8,128)(2,1)S(1)} %copy-done.2, bf16[768,768]{1,0:T(8,128)(2,1)S(1)} %join.1.rest_0_, bf16[768,768]{1,0:T(8,128)(2,1)S(1)} %collective-permute-done.15.rest_1_, ...), custom_call_target="tpu_custom_call" | custom-call | flops 1056964608 | bytes 8388608 | tf_op jit(solution)/shard_map/attend/pallas_call | solution.py:227
  130.3 1.6 collective-permute-start.24
  131.9 5.2 %attend.3.home = bf16[384,384]{1,0:T(8,128)(2,1)S(1)} custom-call(s32[12]{0:T(128)S(1)} %copy-done.3, s32[3,16]{1,0:T(4,128)S(1)} %get-tuple-element.40.ids, bf16[384,384]{1,0:T(8,128)(2,1)S(1)} %copy-done.1, bf16[768,768]{1,0:T(8,128)(2,1)S(1)} %join.1.rest_0_, bf16[768,768]{1,0:T(8,128)(2,1)S(1)} %collective-permute-done.15.rest_1_, ...), custom_call_target="tpu_custom_call" | custom-call | flops 1056964608 | bytes 8388608 | tf_op jit(solution)/shard_map/attend/pallas_call | solution.py:227
  137.1 2.7 %collective-permute-done.24.back = bf16[384,384]{1,0:T(8,128)(2,1)S(1)} collective-permute-done((bf16[384,384]{1,0:T(8,128)(2,1)S(1)}, bf16[384,384]{1,0:T(8,128)(2,1)S(1)}, u32[]{:S(2)}, u32[]{:S(2)}) %collective-permute-start.24) | collective-permute-done | bytes 294944 | tf_op jit(solution)/shard_map/ppermute | solution.py:360
  139.7 3.2 %out_proj.1 = (bf16[384,768]{1,0:T(8,128)(2,1)S(1)}, bf16[384,768]{1,0:T(8,128)(2,1)S(1)}, f32[192,768]{1,0:T(8,128)S(1)}, f32[192,768]{1,0:T(8,128)S(1)}, f32[384,768]{1,0:T(8,128)S(1)}) custom-call(s32[12]{0:T(128)S(1)} %copy-done.3, bf16[384,384]{1,0:T(8,128)(2,1)S(1)} %attend.3.home, bf16[384,384]{1,0:T(8,128)(2,1)S(1)} %collective-permute-done.24.back, ...), custom_call_target="tpu_custom_call" | custom-call | flops 1811939328 | bytes 8388608 | tf_op jit(solution)/shard_map/out_proj/pallas_call | solution.py:265
  143.0 1.9 %collective-permute-start.25 = (bf16[384,768]{1,0:T(8,128)(2,1)S(1)}, bf16[384,768]{1,0:T(8,128)(2,1)S(1)}, u32[]{:S(2)}, u32[]{:S(2)}) collective-permute-start(bf16[384,768]{1,0:T(8,128)(2,1)S(1)} %get-tuple-element.35), channel_id=1, source_target_pairs={{0,4},{4,8},{8,12},{12,0},{1,5},{5,9},{9,13},{13,1},{2,6},{6,10},{... | collective-permute-start | bytes 1769480 | tf_op jit(solution)/shard_map/ppermute | solution.py:325
  144.8 0.2 collective-permute-start.26
  145.1 12.9 %collective-permute-done.25.from_left = bf16[384,768]{1,0:T(8,128)(2,1)S(1)} collective-permute-done((bf16[384,768]{1,0:T(8,128)(2,1)S(1)}, bf16[384,768]{1,0:T(8,128)(2,1)S(1)}, u32[]{:S(2)}, u32[]{:S(2)}) %collective-permute-start.25) | collective-permute-done | bytes 589856 | tf_op jit(solution)/shard_map/ppermute | solution.py:325
  158.0 3.1 %collective-permute-start.27 = (bf16[192,768]{1,0:T(8,128)(2,1)S(1)}, bf16[192,768]{1,0:T(8,128)(2,1)S(1)}, u32[]{:S(2)}, u32[]{:S(2)}) collective-permute-start(bf16[192,768]{1,0:T(8,128)(2,1)S(1)} %add_convert_fusion.1), channel_id=1, source_target_pairs={{0,4},{4,8},{8,12},{12,0},{1,5},{5,9},{9,13},{13,1},{2,6},{6,10},{... | collective-permute-start | bytes 884744 | tf_op jit(solution)/shard_map/ppermute | solution.py:325
  161.0 0.1 add_convert_fusion
  161.1 0.1 collective-permute-start.28
  161.2 5.0 %collective-permute-done.27.left_sum = bf16[192,768]{1,0:T(8,128)(2,1)S(1)} collective-permute-done((bf16[192,768]{1,0:T(8,128)(2,1)S(1)}, bf16[192,768]{1,0:T(8,128)(2,1)S(1)}, u32[]{:S(2)}, u32[]{:S(2)}) %collective-permute-start.27) | collective-permute-done | bytes 294944 | tf_op jit(solution)/shard_map/ppermute | solution.py:325
  166.2 3.6 %collective-permute-done.28.right_sum = bf16[192,768]{1,0:T(8,128)(2,1)S(1)} collective-permute-done((bf16[192,768]{1,0:T(8,128)(2,1)S(1)}, bf16[192,768]{1,0:T(8,128)(2,1)S(1)}, u32[]{:S(2)}, u32[]{:S(2)}) %collective-permute-start.28) | collective-permute-done | bytes 294944 | tf_op jit(solution)/shard_map/ppermute | solution.py:325
  169.8 1.1 last_sum.1
  (47 shorter events, 0.2 us)
Async XLA Ops:
  0.0 2.0 %copy-start = (bf16[768,3,768]{2,0,1:T(8,128)(2,1)S(1)}, bf16[768,3,768]{2,0,1:T(8,128)(2,1)}, u32[]{:S(2)}) copy-start(bf16[768,3,768]{2,0,1:T(8,128)(2,1)} %param.11) | copy-start | bytes 10616836
  0.0 11.1 %copy-start.8 = (s32[3]{0:T(128)S(1)}, s32[3]{0:T(128)}, u32[]{:S(2)}) copy-start(s32[3]{0:T(128)} %param.19) | copy-start | bytes 40
  0.0 11.1 %copy-start.7 = (s32[3,14]{1,0:T(4,128)S(1)}, s32[3,14]{1,0:T(4,128)}, u32[]{:S(2)}) copy-start(s32[3,14]{1,0:T(4,128)} %param.18) | copy-start | bytes 508
  3.2 33.3 %collective-permute-start.9 = (bf16[2,768,384]{2,1,0:T(8,128)(2,1)}, bf16[2,768,384]{2,1,0:T(8,128)(2,1)}, u32[]{:S(2)}, u32[]{:S(2)}) collective-permute-start(bf16[2,768,384]{2,1,0:T(8,128)(2,1)} %dynamic-slice_bitcast_fusion.1), channel_id=1, source_target_pairs={{0,194},{1,195},{2,64},{3,65},{16,210},{17,211},{18,80},{19,81},{3... | collective-permute-start | bytes 3538952 | tf_op jit(solution)/shard_map/ppermute | solution.py:338
  9.0 15.1 %collective-permute-start = (bf16[384,768]{1,0:T(8,128)(2,1)}, bf16[384,768]{1,0:T(8,128)(2,1)}, u32[]{:S(2)}, u32[]{:S(2)}) collective-permute-start(bf16[384,768]{1,0:T(8,128)(2,1)} %x0.1), channel_id=1, source_target_pairs={{0,4},{4,8},{8,12},{12,0},{1,5},{5,9},{9,13},{13,1},{2,6},{6,10},{... | collective-permute-start | bytes 1769480 | tf_op jit(solution)/shard_map/ppermute | solution.py:325
  9.5 17.4 %collective-permute-start.1 = (bf16[384,768]{1,0:T(8,128)(2,1)}, bf16[384,768]{1,0:T(8,128)(2,1)}, u32[]{:S(2)}, u32[]{:S(2)}) collective-permute-start(bf16[384,768]{1,0:T(8,128)(2,1)} %x0.1), channel_id=1, source_target_pairs={{0,12},{4,0},{8,4},{12,8},{1,13},{5,1},{9,5},{13,9},{2,14},{6,2},{... | collective-permute-start | bytes 1769480 | tf_op jit(solution)/shard_map/ppermute | solution.py:325
  13.1 15.2 %collective-permute-start.4 = (bf16[400,768]{1,0:T(8,128)(2,1)}, bf16[400,768]{1,0:T(8,128)(2,1)}, u32[]{:S(2)}, u32[]{:S(2)}) collective-permute-start(bf16[400,768]{1,0:T(8,128)(2,1)} %fusion.1), channel_id=1, source_target_pairs={{0,2},{1,3},{2,0},{3,1},{4,6},{5,7},{6,4},{7,5},{8,10},{9,11},{10,... | collective-permute-start | bytes 1843208 | tf_op jit(solution)/shard_map/ppermute | solution.py:333
  14.6 44.0 %collective-permute-start.7 = (bf16[3,768,384]{2,1,0:T(8,128)(2,1)}, bf16[3,768,384]{2,1,0:T(8,128)(2,1)}, u32[]{:S(2)}, u32[]{:S(2)}) collective-permute-start(bf16[3,768,384]{2,1,0:T(8,128)(2,1)} %dynamic-slice_bitcast_fusion.wo), channel_id=1, source_target_pairs={{0,1},{1,0},{2,3},{3,2},{4,5},{5,4},{6,7},{7,6},{8,9},{9,8},{10,11... | collective-permute-start | bytes 5308424 | tf_op jit(solution)/shard_map/ppermute | solution.py:340
  25.1 7.6 %collective-permute-start.2 = (bf16[192,768]{1,0:T(8,128)(2,1)S(1)}, bf16[192,768]{1,0:T(8,128)(2,1)S(1)}, u32[]{:S(2)}, u32[]{:S(2)}) collective-permute-start(bf16[192,768]{1,0:T(8,128)(2,1)S(1)} %slice.28), channel_id=1, source_target_pairs={{0,4},{4,8},{8,12},{12,0},{1,5},{5,9},{9,13},{13,1},{2,6},{6,10},{... | collective-permute-start | bytes 884744 | tf_op jit(solution)/shard_map/ppermute | solution.py:325
  27.9 8.6 %collective-permute-start.3 = (bf16[192,768]{1,0:T(8,128)(2,1)S(1)}, bf16[192,768]{1,0:T(8,128)(2,1)S(1)}, u32[]{:S(2)}, u32[]{:S(2)}) collective-permute-start(bf16[192,768]{1,0:T(8,128)(2,1)S(1)} %slice.29), channel_id=1, source_target_pairs={{0,12},{4,0},{8,4},{12,8},{1,13},{5,1},{9,5},{13,9},{2,14},{6,2},{... | collective-permute-start | bytes 884744 | tf_op jit(solution)/shard_map/ppermute | solution.py:325
  29.0 13.4 %collective-permute-start.8 = (bf16[1,768,384]{2,1,0:T(8,128)(2,1)S(1)}, bf16[1,768,384]{2,1,0:T(8,128)(2,1)}, u32[]{:S(2)}, u32[]{:S(2)}) collective-permute-start(bf16[1,768,384]{2,1,0:T(8,128)(2,1)S(1)} %dynamic-slice_bitcast_fusion.2), channel_id=1, source_target_pairs={{0,2},{1,3},{2,0},{3,1},{4,6},{5,7},{6,4},{7,5},{8,10},{9,11},{10,... | collective-permute-start | bytes 1769480 | tf_op jit(solution)/shard_map/ppermute | solution.py:339
  32.8 9.7 %copy-start.9 = (bf16[192,768]{1,0:T(8,128)(2,1)}, bf16[192,768]{1,0:T(8,128)(2,1)S(1)}, u32[]{:S(2)}) copy-start(bf16[192,768]{1,0:T(8,128)(2,1)S(1)} %collective-permute-done.2.xt) | copy-start | bytes 884740
  36.4 6.0 %copy-start.10 = (bf16[192,768]{1,0:T(8,128)(2,1)}, bf16[192,768]{1,0:T(8,128)(2,1)S(1)}, u32[]{:S(2)}) copy-start(bf16[192,768]{1,0:T(8,128)(2,1)S(1)} %collective-permute-done.3.xb) | copy-start | bytes 884740
  36.4 22.1 %collective-permute-start.11 = (bf16[2,768,384]{2,1,0:T(8,128)(2,1)}, bf16[2,768,384]{2,1,0:T(8,128)(2,1)}, u32[]{:S(2)}, u32[]{:S(2)}) collective-permute-start(bf16[2,768,384]{2,1,0:T(8,128)(2,1)} %collective-permute-done.9.wzb), channel_id=1, source_target_pairs={{0,1},{1,0},{2,3},{3,2},{4,5},{5,4},{6,7},{7,6},{8,9},{9,8},{10,11... | collective-permute-start | bytes 3538952 | tf_op jit(solution)/shard_map/ppermute | solution.py:345
  36.5 16.6 %collective-permute-start.5 = (bf16[400,768]{1,0:T(8,128)(2,1)}, bf16[400,768]{1,0:T(8,128)(2,1)}, u32[]{:S(2)}, u32[]{:S(2)}) collective-permute-start(bf16[400,768]{1,0:T(8,128)(2,1)} %collective-permute-done.4.x0), channel_id=1, source_target_pairs={{0,4},{4,8},{8,12},{12,0},{1,5},{5,9},{9,13},{13,1},{2,6},{6,10},{... | collective-permute-start | bytes 1843208 | tf_op jit(solution)/shard_map/ppermute | solution.py:325
  36.5 17.7 %collective-permute-start.6 = (bf16[400,768]{1,0:T(8,128)(2,1)}, bf16[400,768]{1,0:T(8,128)(2,1)}, u32[]{:S(2)}, u32[]{:S(2)}) collective-permute-start(bf16[400,768]{1,0:T(8,128)(2,1)} %collective-permute-done.4.x0), channel_id=1, source_target_pairs={{0,12},{4,0},{8,4},{12,8},{1,13},{5,1},{9,5},{13,9},{2,14},{6,2},{... | collective-permute-start | bytes 1843208 | tf_op jit(solution)/shard_map/ppermute | solution.py:325
  42.5 16.1 %collective-permute-start.10 = (bf16[1,768,384]{2,1,0:T(8,128)(2,1)}, bf16[1,768,384]{2,1,0:T(8,128)(2,1)}, u32[]{:S(2)}, u32[]{:S(2)}) collective-permute-start(bf16[1,768,384]{2,1,0:T(8,128)(2,1)} %collective-permute-done.8.wza), channel_id=1, source_target_pairs={{0,1},{1,0},{2,3},{3,2},{4,5},{5,4},{6,7},{7,6},{8,9},{9,8},{10,11... | collective-permute-start | bytes 1769480 | tf_op jit(solution)/shard_map/ppermute | solution.py:345
  55.2 13.7 %collective-permute-start.12 = (bf16[192,768]{1,0:T(8,128)(2,1)S(1)}, bf16[192,768]{1,0:T(8,128)(2,1)S(1)}, u32[]{:S(2)}, u32[]{:S(2)}) collective-permute-start(bf16[192,768]{1,0:T(8,128)(2,1)S(1)} %slice.31), channel_id=1, source_target_pairs={{0,4},{4,8},{8,12},{12,0},{1,5},{5,9},{9,13},{13,1},{2,6},{6,10},{... | collective-permute-start | bytes 884744 | tf_op jit(solution)/shard_map/ppermute | solution.py:325
  56.6 12.4 %collective-permute-start.13 = (bf16[192,768]{1,0:T(8,128)(2,1)S(1)}, bf16[192,768]{1,0:T(8,128)(2,1)S(1)}, u32[]{:S(2)}, u32[]{:S(2)}) collective-permute-start(bf16[192,768]{1,0:T(8,128)(2,1)S(1)} %slice.32), channel_id=1, source_target_pairs={{0,12},{4,0},{8,4},{12,8},{1,13},{5,1},{9,5},{13,9},{2,14},{6,2},{... | collective-permute-start | bytes 884744 | tf_op jit(solution)/shard_map/ppermute | solution.py:325
  68.1 13.4 %copy-start.4 = (bf16[384,768]{1,0:T(8,128)(2,1)S(1)}, bf16[384,768]{1,0:T(8,128)(2,1)}, u32[]{:S(2)}) copy-start(bf16[384,768]{1,0:T(8,128)(2,1)} %get-tuple-element.29.first) | copy-start | bytes 1769476
  68.1 12.6 %collective-permute-start.14 = (bf16[384,768]{1,0:T(8,128)(2,1)}, bf16[384,768]{1,0:T(8,128)(2,1)S(1)}, u32[]{:S(2)}, u32[]{:S(2)}) collective-permute-start(bf16[384,768]{1,0:T(8,128)(2,1)} %get-tuple-element.29.first), channel_id=1, source_target_pairs={{48,0},{112,64},{176,128},{64,112},{128,176},{192,240},{49,1},{113... | collective-permute-start | bytes 1769480 | tf_op jit(solution)/shard_map/ppermute | solution.py:328
  68.9 0.7 copy-start.11
  69.7 0.7 copy-start.12
  79.9 44.0 %copy-start.2 = (bf16[384,384]{1,0:T(8,128)(2,1)S(1)}, bf16[384,384]{1,0:T(8,128)(2,1)}, u32[]{:S(2)}) copy-start(bf16[384,384]{1,0:T(8,128)(2,1)} %get-tuple-element.28.q_ref) | copy-start | bytes 884740
  79.9 44.0 %copy-start.3 = (s32[12]{0:T(128)S(1)}, s32[12]{0:T(128)}, u32[]{:S(2)}) copy-start(s32[12]{0:T(128)} %stack.51.meta) | copy-start | bytes 148
  79.9 15.9 %collective-permute-start.17 = (bf16[384,768]{1,0:T(8,128)(2,1)}, bf16[384,768]{1,0:T(8,128)(2,1)S(1)}, u32[]{:S(2)}, u32[]{:S(2)}) collective-permute-start(bf16[384,768]{1,0:T(8,128)(2,1)} %get-tuple-element.30.second), channel_id=1, source_target_pairs={{48,64},{112,128},{176,192},{64,48},{128,112},{192,176},{49,65},{1... | collective-permute-start | bytes 1769480 | tf_op jit(solution)/shard_map/ppermute | solution.py:328
  80.7 15.2 %collective-permute-start.16 = (bf16[384,768]{1,0:T(8,128)(2,1)S(1)}, bf16[384,768]{1,0:T(8,128)(2,1)S(1)}, u32[]{:S(2)}, u32[]{:S(2)}) collective-permute-start(bf16[384,768]{1,0:T(8,128)(2,1)S(1)} %collective-permute-done.14.crossed), channel_id=1, source_target_pairs={{0,64},{64,128},{128,192},{112,48},{176,112},{240,176},{1,65},{65,... | collective-permute-start | bytes 1769480 | tf_op jit(solution)/shard_map/ppermute | solution.py:328
  81.5 1.1 copy-start.5
  82.8 35.3 %collective-permute-start.15 = (bf16[768,768]{1,0:T(8,128)(2,1)S(1)}, bf16[768,768]{1,0:T(8,128)(2,1)S(1)}, u32[]{:S(2)}, u32[]{:S(2)}) collective-permute-start(bf16[768,768]{1,0:T(8,128)(2,1)S(1)} %join.1.rest_0_), channel_id=1, source_target_pairs={{0,16},{16,32},{32,48},{64,80},{80,96},{96,112},{128,144},{144,160... | collective-permute-start | bytes 3538952 | tf_op jit(solution)/shard_map/ppermute | solution.py:328
  86.3 33.0 %collective-permute-start.20 = (bf16[768,768]{1,0:T(8,128)(2,1)S(1)}, bf16[768,768]{1,0:T(8,128)(2,1)S(1)}, u32[]{:S(2)}, u32[]{:S(2)}) collective-permute-start(bf16[768,768]{1,0:T(8,128)(2,1)S(1)} %join.1.rest_0_), channel_id=1, source_target_pairs={{16,0},{32,16},{48,32},{80,64},{96,80},{112,96},{144,128},{160,144... | collective-permute-start | bytes 3538952 | tf_op jit(solution)/shard_map/ppermute | solution.py:328
  95.8 2.1 %collective-permute-start.19 = (bf16[384,768]{1,0:T(8,128)(2,1)S(1)}, bf16[384,768]{1,0:T(8,128)(2,1)S(1)}, u32[]{:S(2)}, u32[]{:S(2)}) collective-permute-start(bf16[384,768]{1,0:T(8,128)(2,1)S(1)} %collective-permute-done.17.rest_4_), channel_id=1, source_target_pairs={{0,1},{1,0},{2,3},{3,2},{4,5},{5,4},{6,7},{7,6},{8,9},{9,8},{10,11... | collective-permute-start | bytes 1769480 | tf_op jit(solution)/shard_map/ppermute | solution.py:356
  95.9 2.8 %collective-permute-start.18 = (bf16[384,768]{1,0:T(8,128)(2,1)S(1)}, bf16[384,768]{1,0:T(8,128)(2,1)S(1)}, u32[]{:S(2)}, u32[]{:S(2)}) collective-permute-start(bf16[384,768]{1,0:T(8,128)(2,1)S(1)} %collective-permute-done.16.rest_3_), channel_id=1, source_target_pairs={{0,1},{1,0},{2,3},{3,2},{4,5},{5,4},{6,7},{7,6},{8,9},{9,8},{10,11... | collective-permute-start | bytes 1769480 | tf_op jit(solution)/shard_map/ppermute | solution.py:356
  96.4 23.4 %collective-permute-start.21 = (bf16[768,768]{1,0:T(8,128)(2,1)S(1)}, bf16[768,768]{1,0:T(8,128)(2,1)S(1)}, u32[]{:S(2)}, u32[]{:S(2)}) collective-permute-start(bf16[768,768]{1,0:T(8,128)(2,1)S(1)} %join.1.rest_0_), channel_id=1, source_target_pairs={{0,1},{1,0},{2,3},{3,2},{4,5},{5,4},{6,7},{7,6},{8,9},{9,8},{10,11... | collective-permute-start | bytes 3538952 | tf_op jit(solution)/shard_map/ppermute | solution.py:358
  119.3 2.8 %collective-permute-start.22 = (bf16[768,768]{1,0:T(8,128)(2,1)S(1)}, bf16[768,768]{1,0:T(8,128)(2,1)S(1)}, u32[]{:S(2)}, u32[]{:S(2)}) collective-permute-start(bf16[768,768]{1,0:T(8,128)(2,1)S(1)} %collective-permute-done.15.rest_1_), channel_id=1, source_target_pairs={{0,1},{1,0},{2,3},{3,2},{4,5},{5,4},{6,7},{7,6},{8,9},{9,8},{10,11... | collective-permute-start | bytes 3538952 | tf_op jit(solution)/shard_map/ppermute | solution.py:358
  119.3 4.5 %collective-permute-start.23 = (bf16[768,768]{1,0:T(8,128)(2,1)S(1)}, bf16[768,768]{1,0:T(8,128)(2,1)S(1)}, u32[]{:S(2)}, u32[]{:S(2)}) collective-permute-start(bf16[768,768]{1,0:T(8,128)(2,1)S(1)} %collective-permute-done.20.rest_2_), channel_id=1, source_target_pairs={{0,1},{1,0},{2,3},{3,2},{4,5},{5,4},{6,7},{7,6},{8,9},{9,8},{10,11... | collective-permute-start | bytes 3538952 | tf_op jit(solution)/shard_map/ppermute | solution.py:358
  123.9 8.0 %copy-start.1 = (bf16[384,384]{1,0:T(8,128)(2,1)S(1)}, bf16[384,384]{1,0:T(8,128)(2,1)}, u32[]{:S(2)}) copy-start(bf16[384,384]{1,0:T(8,128)(2,1)} %get-tuple-element.33.q_ref) | copy-start | bytes 884740
  123.9 15.9 %slice-start = ((s8[4718592]{0:T(1024)(128)(4,1)}), s8[4194304]{0:T(1024)(128)(4,1)S(1)}, s32[]{:S(2)}) async-start(s8[4718592]{0:T(1024)(128)(4,1)} %bitcast.23), calls=%async_computation | async-start | bytes 8388608
  130.3 9.4 %collective-permute-start.24 = (bf16[384,384]{1,0:T(8,128)(2,1)S(1)}, bf16[384,384]{1,0:T(8,128)(2,1)S(1)}, u32[]{:S(2)}, u32[]{:S(2)}) collective-permute-start(bf16[384,384]{1,0:T(8,128)(2,1)S(1)} %attend.2), channel_id=1, source_target_pairs={{0,2},{1,3},{2,0},{3,1},{4,6},{5,7},{6,4},{7,5},{8,10},{9,11},{10,... | collective-permute-start | bytes 884744 | tf_op jit(solution)/shard_map/ppermute | solution.py:360
  131.9 7.8 %slice-start.1 = ((s8[4718592]{0:T(1024)(128)(4,1)}), s8[524288]{0:T(1024)(128)(4,1)S(1)}, s32[]{:S(2)}) async-start(s8[4718592]{0:T(1024)(128)(4,1)} %bitcast.23), calls=%async_computation.1 | async-start | bytes 1048576
  142.9 18.3 %copy-start.6 = (f32[768]{0:T(1024)S(1)}, f32[768]{0:T(1024)}, u32[]{:S(2)}) copy-start(f32[768]{0:T(1024)} %param.15) | copy-start | bytes 9220
  143.0 15.0 %collective-permute-start.25 = (bf16[384,768]{1,0:T(8,128)(2,1)S(1)}, bf16[384,768]{1,0:T(8,128)(2,1)S(1)}, u32[]{:S(2)}, u32[]{:S(2)}) collective-permute-start(bf16[384,768]{1,0:T(8,128)(2,1)S(1)} %get-tuple-element.35), channel_id=1, source_target_pairs={{0,4},{4,8},{8,12},{12,0},{1,5},{5,9},{9,13},{13,1},{2,6},{6,10},{... | collective-permute-start | bytes 1769480 | tf_op jit(solution)/shard_map/ppermute | solution.py:325
  144.8 16.2 %collective-permute-start.26 = (bf16[384,768]{1,0:T(8,128)(2,1)S(1)}, bf16[384,768]{1,0:T(8,128)(2,1)S(1)}, u32[]{:S(2)}, u32[]{:S(2)}) collective-permute-start(bf16[384,768]{1,0:T(8,128)(2,1)S(1)} %get-tuple-element.36), channel_id=1, source_target_pairs={{0,12},{4,0},{8,4},{12,8},{1,13},{5,1},{9,5},{13,9},{2,14},{6,2},{... | collective-permute-start | bytes 1769480 | tf_op jit(solution)/shard_map/ppermute | solution.py:325
  158.0 8.2 %collective-permute-start.27 = (bf16[192,768]{1,0:T(8,128)(2,1)S(1)}, bf16[192,768]{1,0:T(8,128)(2,1)S(1)}, u32[]{:S(2)}, u32[]{:S(2)}) collective-permute-start(bf16[192,768]{1,0:T(8,128)(2,1)S(1)} %add_convert_fusion.1), channel_id=1, source_target_pairs={{0,4},{4,8},{8,12},{12,0},{1,5},{5,9},{9,13},{13,1},{2,6},{6,10},{... | collective-permute-start | bytes 884744 | tf_op jit(solution)/shard_map/ppermute | solution.py:325
  161.1 8.7 %collective-permute-start.28 = (bf16[192,768]{1,0:T(8,128)(2,1)S(1)}, bf16[192,768]{1,0:T(8,128)(2,1)S(1)}, u32[]{:S(2)}, u32[]{:S(2)}) collective-permute-start(bf16[192,768]{1,0:T(8,128)(2,1)S(1)} %add_convert_fusion), channel_id=1, source_target_pairs={{0,12},{4,0},{8,4},{12,8},{1,13},{5,1},{9,5},{13,9},{2,14},{6,2},{... | collective-permute-start | bytes 884744 | tf_op jit(solution)/shard_map/ppermute | solution.py:325
